TPU v7x, 768 devices: a whole 4x8x12 slice. The times are simulated.
768 devices in a mesh: row: 4 (over x), col: 96 (over z, y), layer: 2 (over core).
Axes of the slice: x: 4, y: 8, z: 12, core: 2. Of those that a mesh axis runs over, the one named last changes fastest.
Arguments:
- values: bfloat16 [1536, 10, 128, 128], P(('row', 'col'), None, 'layer'), may hold values from -0.8984375 to 0.8984375
- columns: int32 [1536, 10], replicated, may hold values from 0 to 1535, as said below
Outputs:
- square: bfloat16 [1536, 10, 128, 128], P(('row', 'col'), None, 'layer')
Inputs may be any that keep to these rules, and one draw needn't show every extreme that they name: `columns`: each row's 10 entries are distinct, and each lies within 12 of the row's index, counted cyclically modulo 1536.
All inputs are finite; a program needn't handle non-finite values.
Results may differ from a plain program's by a relative error of at most 0.001.
Values may be sent and summed in bfloat16 or wider, within the bound.
A program may use at most 64 MiB of HBM per device.

v0:
```python
import jax
import jax.numpy as jnp
from jax import lax
from jax.sharding import PartitionSpec as P


def shifted(value, axis, steps):
    count = lax.axis_size(axis)
    pairs = [(source, (source + steps) % count) for source in range(count)]
    return lax.ppermute(value, axis, pairs)


def fetch_direct(values, offset):
    return shifted(values, ("row", "col"), -offset)


def select_blocks(piece, flat_index, rows_here, slots):
    count = piece.shape[2]
    width = piece.shape[3]
    flat_piece = piece.reshape(7 * rows_here * slots, count, width)
    flat_piece = jnp.concatenate([flat_piece, jnp.zeros((1, count, width), piece.dtype)], axis=0)
    return jnp.take(flat_piece, flat_index, axis=0).reshape(rows_here, slots, slots, count, width)


def on_device(values, columns):
    rows_here, slots, narrow, width = values.shape
    devices_along = lax.axis_size(("row", "col"))
    total_rows = rows_here * devices_along
    position = lax.axis_index(("row", "col"))
    first_row = position * rows_here
    own_columns = lax.dynamic_slice_in_dim(columns, first_row, rows_here, 0)
    nearby = {0: values}
    for offset in (-3, -2, -1, 1, 2, 3):
        nearby[offset] = fetch_direct(values, offset)
    near_values = jnp.concatenate([nearby[offset] for offset in range(-3, 4)], axis=0)
    local_row = (own_columns - first_row + 3 * rows_here) % total_rows
    block_columns = columns[own_columns]
    matches = block_columns[:, :, :, None] == own_columns[:, None, None, :]
    slot_range = jnp.arange(slots, dtype=jnp.int32)
    slot_index = jnp.sum(jnp.where(matches, slot_range[None, None, :, None], 0), axis=2)
    present = jnp.any(matches, axis=2)
    empty_index = 7 * rows_here * slots
    flat_index = jnp.where(
        present, local_row[:, :, None] * slots + slot_index, empty_index
    ).reshape(-1)
    chosen = select_blocks(
        lax.all_gather(near_values, "layer", axis=2, tiled=True), flat_index, rows_here, slots
    )
    result = jnp.einsum("ikab,ikmbc->imac", values, chosen, preferred_element_type=jnp.float32)
    return result.astype(jnp.bfloat16)


def solution(mesh):
    return jax.shard_map(
        on_device,
        mesh=mesh,
        in_specs=(P(("row", "col"), None, "layer", None), P()),
        out_specs=P(("row", "col"), None, "layer", None),
        check_vma=False,
    )
```

profile of v0, /device:TPU:1, one launch (start us, length us, event | category | flops | bytes accessed | tf_op | source)
XLA Modules:
  0.0 207.2 jit_solution(7982787214457328913)
XLA Ops:
  6.5 6.0 %collective-permute-start = (bf16[4,10,64,128]{3,2,1,0:T(8,128)(2,1)}, bf16[4,10,64,128]{3,2,1,0:T(8,128)(2,1)S(1)}, u32[]{:S(2)}, u32[]{:S(2)}) collective-permute-start(bf16[4,10,64,128]{3,2,1,0:T(8,128)(2,1)} %param.2), channel_id=1, source_target_pairs={{0,6},{2,8},{4,10},{6,12},{8,14},{10,16},{12,18},{14,20},{16,22},{... | collective-permute-start | bytes 1966088 | tf_op jit(solution)/shard_map/ppermute | solution.py:10
  12.6 4.5 %collective-permute-start.1 = (bf16[4,10,64,128]{3,2,1,0:T(8,128)(2,1)}, bf16[4,10,64,128]{3,2,1,0:T(8,128)(2,1)S(1)}, u32[]{:S(2)}, u32[]{:S(2)}) collective-permute-start(bf16[4,10,64,128]{3,2,1,0:T(8,128)(2,1)} %param.2), channel_id=1, source_target_pairs={{0,4},{2,6},{4,8},{6,10},{8,12},{10,14},{12,16},{14,18},{16,20},{1... | collective-permute-start | bytes 1966088 | tf_op jit(solution)/shard_map/ppermute | solution.py:10
  17.1 2.3 %collective-permute-start.2 = (bf16[4,10,64,128]{3,2,1,0:T(8,128)(2,1)}, bf16[4,10,64,128]{3,2,1,0:T(8,128)(2,1)S(1)}, u32[]{:S(2)}, u32[]{:S(2)}) collective-permute-start(bf16[4,10,64,128]{3,2,1,0:T(8,128)(2,1)} %param.2), channel_id=1, source_target_pairs={{0,2},{2,4},{4,6},{6,8},{8,10},{10,12},{12,14},{14,16},{16,18},{18... | collective-permute-start | bytes 1966088 | tf_op jit(solution)/shard_map/ppermute | solution.py:10
  19.4 13.1 %collective-permute-start.3 = (bf16[4,10,64,128]{3,2,1,0:T(8,128)(2,1)}, bf16[4,10,64,128]{3,2,1,0:T(8,128)(2,1)S(1)}, u32[]{:S(2)}, u32[]{:S(2)}) collective-permute-start(bf16[4,10,64,128]{3,2,1,0:T(8,128)(2,1)} %param.2), channel_id=1, source_target_pairs={{0,766},{2,0},{4,2},{6,4},{8,6},{10,8},{12,10},{14,12},{16,14},{18... | collective-permute-start | bytes 1966088 | tf_op jit(solution)/shard_map/ppermute | solution.py:10
  32.6 4.3 %collective-permute-start.4 = (bf16[4,10,64,128]{3,2,1,0:T(8,128)(2,1)}, bf16[4,10,64,128]{3,2,1,0:T(8,128)(2,1)S(1)}, u32[]{:S(2)}, u32[]{:S(2)}) collective-permute-start(bf16[4,10,64,128]{3,2,1,0:T(8,128)(2,1)} %param.2), channel_id=1, source_target_pairs={{0,764},{2,766},{4,0},{6,2},{8,4},{10,6},{12,8},{14,10},{16,12},{1... | collective-permute-start | bytes 1966088 | tf_op jit(solution)/shard_map/ppermute | solution.py:10
  36.8 45.0 %collective-permute-done = bf16[4,10,64,128]{3,2,1,0:T(8,128)(2,1)S(1)} collective-permute-done((bf16[4,10,64,128]{3,2,1,0:T(8,128)(2,1)}, bf16[4,10,64,128]{3,2,1,0:T(8,128)(2,1)S(1)}, u32[]{:S(2)}, u32[]{:S(2)}) %collective-permute-start) | collective-permute-done | bytes 655392 | tf_op jit(solution)/shard_map/ppermute | solution.py:10
  81.8 1.9 collective-permute-start.5
  83.7 0.9 constant_dynamic-update-slice_fusion.6
  84.6 18.7 %collective-permute-done.1 = bf16[4,10,64,128]{3,2,1,0:T(8,128)(2,1)S(1)} collective-permute-done((bf16[4,10,64,128]{3,2,1,0:T(8,128)(2,1)}, bf16[4,10,64,128]{3,2,1,0:T(8,128)(2,1)S(1)}, u32[]{:S(2)}, u32[]{:S(2)}) %collective-permute-start.1) | collective-permute-done | bytes 655392 | tf_op jit(solution)/shard_map/ppermute | solution.py:10
  103.3 0.9 constant_dynamic-update-slice_fusion.5
  104.2 7.5 %collective-permute-done.2 = bf16[4,10,64,128]{3,2,1,0:T(8,128)(2,1)S(1)} collective-permute-done((bf16[4,10,64,128]{3,2,1,0:T(8,128)(2,1)}, bf16[4,10,64,128]{3,2,1,0:T(8,128)(2,1)S(1)}, u32[]{:S(2)}, u32[]{:S(2)}) %collective-permute-start.2) | collective-permute-done | bytes 655392 | tf_op jit(solution)/shard_map/ppermute | solution.py:10
  111.6 0.9 constant_dynamic-update-slice_fusion.4
  112.5 2.0 constant_dynamic-update-slice_fusion.3
  114.5 0.9 constant_dynamic-update-slice_fusion.2
  115.4 0.9 constant_dynamic-update-slice_fusion.1
  116.3 22.9 %collective-permute-done.5 = bf16[4,10,64,128]{3,2,1,0:T(8,128)(2,1)S(1)} collective-permute-done((bf16[4,10,64,128]{3,2,1,0:T(8,128)(2,1)}, bf16[4,10,64,128]{3,2,1,0:T(8,128)(2,1)S(1)}, u32[]{:S(2)}, u32[]{:S(2)}) %collective-permute-start.5) | collective-permute-done | bytes 655392 | tf_op jit(solution)/shard_map/ppermute | solution.py:10
  139.2 0.9 constant_dynamic-update-slice_fusion
  140.2 0.3 copy.15
  140.5 0.1 fusion.15
  140.6 0.1 copy.18
  140.7 0.1 copy.14
  140.7 0.1 reshape.66
  140.8 0.6 gather_fusion
  141.4 0.2 copy.17
  141.6 0.2 fusion.14
  141.8 0.2 compare_reduce_fusion
  141.9 0.1 compare_and_fusion
  142.1 0.1 select_n.63
  142.2 23.7 %all-gather.2.cloned.1.call-done = bf16[28,10,128,128]{3,2,1,0:T(8,128)(2,1)} async-done(((bf16[28,10,64,128]{3,2,1,0:T(8,128)(2,1)}), bf16[28,10,128,128]{3,2,1,0:T(8,128)(2,1)}) %all-gather.2.cloned.1.call-update) | async-done | bytes 9175056 | tf_op jit(solution)/shard_map/all_gather | solution.py:47
  165.9 11.3 %concatenate.7 = bf16[281,128,128]{2,1,0:T(8,128)(2,1)} pad(bf16[280,128,128]{2,1,0:T(8,128)(2,1)} %bitcast.22, bf16[]{:T(256)} %constant.51.clone.1), padding=0_1x0_0x0_0 | pad | bytes 18382850 | tf_op jit(solution)/shard_map/concatenate | solution.py:21
  177.2 15.9 %gather_fusion.1 = bf16[400,128,128]{2,1,0:T(8,128)(2,1)} fusion(bf16[281,128,128]{2,1,0:T(8,128)(2,1)} %concatenate.7, s32[1024]{0:T(1024)S(1)} %pad_clamp_fusion), kind=kCustom, calls=%fused_computation.1 | custom fusion | bytes 26216000 | tf_op jit(solution)/shard_map/jit(_take)/gather | solution.py:22
  193.1 7.3 %fusion.10 = bf16[4,10,64,128]{3,2,1,0:T(8,128)(2,1)} fusion(bf16[4,10,10,128,128]{4,3,2,1,0:T(8,128)(2,1)} %bitcast.21, pred[4,10,10]{2,1,0:T(8,128)(4,1)S(1)} %copy.19, bf16[4,10,64,128]{3,2,1,0:T(8,128)(2,1)S(1)} %copy-done), kind=kOutput, calls=%fused_computation.8 | convolution fusion | flops 845742080 | bytes 14418320 | tf_op jit(solution)/shard_map/ikab,ikmbc->imac/dot_general | solution.py:49
  (15 shorter events, 0.1 us)
Async XLA Ops:
  6.5 159.3 %all-gather.2.cloned.1.call-start = ((), (), s32[]{:S(2)}) async-start(), calls=%async_computation | async-start | bytes 13762560 | tf_op jit(solution)/shard_map/all_gather | solution.py:47
  6.5 75.3 %collective-permute-start = (bf16[4,10,64,128]{3,2,1,0:T(8,128)(2,1)}, bf16[4,10,64,128]{3,2,1,0:T(8,128)(2,1)S(1)}, u32[]{:S(2)}, u32[]{:S(2)}) collective-permute-start(bf16[4,10,64,128]{3,2,1,0:T(8,128)(2,1)} %param.2), channel_id=1, source_target_pairs={{0,6},{2,8},{4,10},{6,12},{8,14},{10,16},{12,18},{14,20},{16,22},{... | collective-permute-start | bytes 1966088 | tf_op jit(solution)/shard_map/ppermute | solution.py:10
  12.6 90.7 %collective-permute-start.1 = (bf16[4,10,64,128]{3,2,1,0:T(8,128)(2,1)}, bf16[4,10,64,128]{3,2,1,0:T(8,128)(2,1)S(1)}, u32[]{:S(2)}, u32[]{:S(2)}) collective-permute-start(bf16[4,10,64,128]{3,2,1,0:T(8,128)(2,1)} %param.2), channel_id=1, source_target_pairs={{0,4},{2,6},{4,8},{6,10},{8,12},{10,14},{12,16},{14,18},{16,20},{1... | collective-permute-start | bytes 1966088 | tf_op jit(solution)/shard_map/ppermute | solution.py:10
  17.1 94.5 %collective-permute-start.2 = (bf16[4,10,64,128]{3,2,1,0:T(8,128)(2,1)}, bf16[4,10,64,128]{3,2,1,0:T(8,128)(2,1)S(1)}, u32[]{:S(2)}, u32[]{:S(2)}) collective-permute-start(bf16[4,10,64,128]{3,2,1,0:T(8,128)(2,1)} %param.2), channel_id=1, source_target_pairs={{0,2},{2,4},{4,6},{6,8},{8,10},{10,12},{12,14},{14,16},{16,18},{18... | collective-permute-start | bytes 1966088 | tf_op jit(solution)/shard_map/ppermute | solution.py:10
  19.4 95.0 %collective-permute-start.3 = (bf16[4,10,64,128]{3,2,1,0:T(8,128)(2,1)}, bf16[4,10,64,128]{3,2,1,0:T(8,128)(2,1)S(1)}, u32[]{:S(2)}, u32[]{:S(2)}) collective-permute-start(bf16[4,10,64,128]{3,2,1,0:T(8,128)(2,1)} %param.2), channel_id=1, source_target_pairs={{0,766},{2,0},{4,2},{6,4},{8,6},{10,8},{12,10},{14,12},{16,14},{18... | collective-permute-start | bytes 1966088 | tf_op jit(solution)/shard_map/ppermute | solution.py:10
  32.6 82.8 %collective-permute-start.4 = (bf16[4,10,64,128]{3,2,1,0:T(8,128)(2,1)}, bf16[4,10,64,128]{3,2,1,0:T(8,128)(2,1)S(1)}, u32[]{:S(2)}, u32[]{:S(2)}) collective-permute-start(bf16[4,10,64,128]{3,2,1,0:T(8,128)(2,1)} %param.2), channel_id=1, source_target_pairs={{0,764},{2,766},{4,0},{6,2},{8,4},{10,6},{12,8},{14,10},{16,12},{1... | collective-permute-start | bytes 1966088 | tf_op jit(solution)/shard_map/ppermute | solution.py:10
  81.8 57.4 %collective-permute-start.5 = (bf16[4,10,64,128]{3,2,1,0:T(8,128)(2,1)}, bf16[4,10,64,128]{3,2,1,0:T(8,128)(2,1)S(1)}, u32[]{:S(2)}, u32[]{:S(2)}) collective-permute-start(bf16[4,10,64,128]{3,2,1,0:T(8,128)(2,1)} %param.2), channel_id=1, source_target_pairs={{0,762},{2,764},{4,766},{6,0},{8,2},{10,4},{12,6},{14,8},{16,10},{... | collective-permute-start | bytes 1966088 | tf_op jit(solution)/shard_map/ppermute | solution.py:10
  114.5 25.7 %copy-start.1 = (s32[1536,10]{0,1:T(8,128)S(1)}, s32[1536,10]{0,1:T(8,128)}, u32[]{:S(2)}) copy-start(s32[1536,10]{0,1:T(8,128)} %param.3) | copy-start | bytes 184324
  177.2 15.9 %copy-start = (bf16[4,10,64,128]{3,2,1,0:T(8,128)(2,1)S(1)}, bf16[4,10,64,128]{3,2,1,0:T(8,128)(2,1)}, u32[]{:S(2)}) copy-start(bf16[4,10,64,128]{3,2,1,0:T(8,128)(2,1)} %param.2) | copy-start | bytes 1966084
Sparse Core Ops, SparseCore 0:
  140.3 25.5 all-gather.1
where the time goes:
time: 208 us; the launch traced here: 207 us
  waiting for transfers between devices  118 us (57%)
  local copies, waits for them, and re-layouts  35.9 us (17%)
  starting transfers between devices  32.2 us (15%)
  between operations  13.5 us (6%)
  matrix products  7.32 us (4%)
    ppermute x6, waiting for transfers between devices, shifted(): return lax.ppermute(value, axis, pairs)  94 us
    ppermute x6, starting transfers between devices, shifted(): return lax.ppermute(value, axis, pairs)  32.2 us
    all_gather x1, waiting for transfers between devices, on_device(): lax.all_gather(near_values, 'layer', axis=2, tiled=True)  23.7 us
    gather x1, local copies, waits for them, and re-layouts, select_blocks(): jnp.take(flat_piece, flat_index, axis=0)  15.9 us
    concatenate x1, local copies, waits for them, and re-layouts, select_blocks(): jnp.concatenate([flat_piece, jnp.zeros((1, count, width), piece.dtype)],...  11.3 us
    dot_general x1, matrix products, on_device(): jnp.einsum('ikab,ikmbc->imac', values, chosen, preferred_element_type=jnp...  7.32 us
    unnamed x11, local copies, waits for them, and re-layouts  6.69 us
  transfers between devices with their start and end apart: 7, of which 5 were waited for; matrix products, arithmetic and copies ran while one was open for 4% of the time, Pallas kernels for 0%

commit v1 on v0

v1 whole, which is shorter than its diff:
```python
import functools

import jax
import jax.numpy as jnp
from jax import lax
from jax.experimental import pallas as pl
from jax.experimental.pallas import tpu as pltpu
from jax.sharding import PartitionSpec as P

HOPS = 3


def square_kernel(sizes, columns_ref, values_ref, out_ref, near, own, table, place,
                  hop_send, hop_recv, core_send, core_recv, local_sem):
    rows_axis, cols_axis = sizes
    positions = rows_axis * cols_axis
    rows_here, slots, half, width = values_ref.shape
    total_rows = rows_here * positions
    row, col, layer = lax.axis_index("row"), lax.axis_index("col"), lax.axis_index("layer")
    position = row * cols_axis + col
    units = 2 * HOPS + 1
    empty = units * rows_here * slots

    def at(offset):
        there = lax.rem(position + offset + positions, positions)
        return (there // cols_axis, lax.rem(there, cols_axis), layer)

    sibling = (row, col, 1 - layer)
    my_half = pl.ds(pl.multiple_of(layer * half, half), half)

    def unit_rows(unit, r):
        return near.at[pl.ds((unit * rows_here + r) * slots, slots), my_half, :]

    def hop(h, direction, r):
        index = 0 if direction > 0 else 1
        source = values_ref.at[r] if h == 0 else unit_rows(HOPS - direction * h, r)
        return pltpu.make_async_remote_copy(
            source, unit_rows(HOPS - direction * (h + 1), r),
            hop_send.at[h, index, r], hop_recv.at[h, index, r],
            device_id=at(direction), device_id_type=pl.DeviceIdType.MESH)

    def across(unit, r):
        source = values_ref.at[r] if unit == HOPS else unit_rows(unit, r)
        return pltpu.make_async_remote_copy(
            source, unit_rows(unit, r), core_send.at[unit, r], core_recv.at[unit, r],
            device_id=sibling, device_id_type=pl.DeviceIdType.MESH)

    table_copy = pltpu.make_async_copy(columns_ref, table, local_sem.at[0])
    own_copy = pltpu.make_async_copy(values_ref, own, local_sem.at[1])
    table_copy.start()
    own_copy.start()

    barrier = pltpu.get_barrier_semaphore()
    for peer in (at(1), at(-1), sibling):
        pl.semaphore_signal(barrier, inc=1, device_id=peer, device_id_type=pl.DeviceIdType.MESH)
    pl.semaphore_wait(barrier, 3)

    for r in range(rows_here):
        for direction in (1, -1):
            hop(0, direction, r).start()
    for r in range(rows_here):
        across(HOPS, r).start()
    near[empty] = jnp.zeros((2 * half, width), near.dtype)
    near_own = [pltpu.make_async_copy(values_ref.at[r], unit_rows(HOPS, r), local_sem.at[2 + r]) for r in range(rows_here)]
    for copy in near_own:
        copy.start()
    table_copy.wait()

    @pl.loop(0, rows_here * slots)
    def _(step):
        t, k = step // slots, lax.rem(step, slots)
        i = position * rows_here + t
        j = table[k, i]
        base = lax.rem(j - position * rows_here + HOPS * rows_here + total_rows, total_rows) * slots
        there = [table[s, j] for s in range(slots)]
        for m in range(slots):
            wanted = table[m, i]
            found = empty
            for s in range(slots):
                found = jnp.where(there[s] == wanted, base + s, found)
            place[step * slots + m] = jnp.minimum(found, empty)

    for h in range(HOPS):
        for r in range(rows_here):
            for direction in (1, -1):
                hop(h, direction, r).wait_recv()
                if h + 1 < HOPS:
                    hop(h + 1, direction, r).start()
                across(HOPS - direction * (h + 1), r).start()
    own_copy.wait()
    for copy in near_own:
        copy.wait()
    for unit in range(units):
        for r in range(rows_here):
            across(unit, r).wait_recv()

    pairs = slots // 2

    @pl.loop(0, rows_here * pairs)
    def _(step):
        t, pair = step // pairs, lax.rem(step, pairs)
        left = jnp.concatenate([own[t, k] for k in range(slots)], axis=1)
        first = t * slots * slots + 2 * pair
        right = jnp.concatenate([
            jnp.concatenate([near[place[first + k * slots]], near[place[first + k * slots + 1]]], axis=1)
            for k in range(slots)], axis=0)
        product = jnp.dot(left, right, preferred_element_type=jnp.float32).astype(out_ref.dtype)
        out_ref[t, 2 * pair] = product[:, :width]
        out_ref[t, 2 * pair + 1] = product[:, width:]

    for h in range(HOPS):
        for r in range(rows_here):
            for direction in (1, -1):
                hop(h, direction, r).wait_send()
    for unit in range(units):
        for r in range(rows_here):
            across(unit, r).wait_send()


def on_device(sizes, values, columns):
    rows_here, slots, half, width = values.shape
    units = 2 * HOPS + 1
    return pl.pallas_call(
        functools.partial(square_kernel, sizes),
        out_shape=jax.ShapeDtypeStruct(values.shape, values.dtype),
        in_specs=[pl.BlockSpec(memory_space=pltpu.HBM), pl.BlockSpec(memory_space=pltpu.HBM)],
        out_specs=pl.BlockSpec(memory_space=pltpu.VMEM),
        scratch_shapes=[
            pltpu.VMEM((units * rows_here * slots + 1, 2 * half, width), values.dtype),
            pltpu.VMEM(values.shape, values.dtype),
            pltpu.SMEM(columns.shape[::-1], jnp.int32),
            pltpu.SMEM((rows_here * slots * slots,), jnp.int32),
            pltpu.SemaphoreType.DMA((HOPS, 2, rows_here)),
            pltpu.SemaphoreType.DMA((HOPS, 2, rows_here)),
            pltpu.SemaphoreType.DMA((units, rows_here)),
            pltpu.SemaphoreType.DMA((units, rows_here)),
            pltpu.SemaphoreType.DMA((2 + rows_here,)),
        ],
        compiler_params=pltpu.CompilerParams(
            collective_id=0, has_side_effects=True, vmem_limit_bytes=32 << 20),
        name="square",
    )(columns.T, values)


def solution(mesh):
    return jax.shard_map(
        functools.partial(on_device, (mesh.shape["row"], mesh.shape["col"])),
        mesh=mesh,
        in_specs=(P(("row", "col"), None, "layer", None), P()),
        out_specs=P(("row", "col"), None, "layer", None),
        check_vma=False,
    )
```

time: 208 us -> 74.3 us (0.36)
  waiting for transfers between devices: 118 us -> 0 us
  Pallas kernels: 0 us -> 71.3 us
  local copies, waits for them, and re-layouts: 35.9 us -> 2.82 us
  starting transfers between devices: 32.2 us -> 0 us
  between operations: 13.5 us -> 0.01 us
  matrix products: 7.32 us -> 0 us
    ppermute x6 -> x0, waiting for transfers between devices: 94 us -> none  [shifted(): return lax.ppermute(value, axis, pairs)]
    pallas_call x0 -> x1, Pallas kernels: none -> 71.3 us  [on_device(): pl.pallas_call(functools.partial(square_kernel, sizes), out_shape=jax.Sha...]
    ppermute x6 -> x0, starting transfers between devices: 32.2 us -> none  [shifted(): return lax.ppermute(value, axis, pairs)]
    all_gather x1 -> x0, waiting for transfers between devices: 23.7 us -> none  [on_device(): lax.all_gather(near_values, 'layer', axis=2, tiled=True)]
    gather x4 -> x0, local copies, waits for them, and re-layouts: 16.7 us -> none  [the longest x1 15.9 us: select_blocks(): jnp.take(flat_piece, flat_index, axis=0)]
    concatenate x2 -> x0, local copies, waits for them, and re-layouts: 12.2 us -> none  [the longest x1 11.3 us: select_blocks(): jnp.concatenate([flat_piece, jnp.zeros((1, count, width), piece.dtype)],...]
    dot_general x1 -> x0, matrix products: 7.32 us -> none  [on_device(): jnp.einsum('ikab,ikmbc->imac', values, chosen, preferred_element_type=jnp...]
    unnamed x11 -> x5, local copies, waits for them, and re-layouts: 6.69 us -> 2.82 us
  transfers between devices with their start and end apart: 7 -> 0, of which waited for: 5 -> 0; matrix products, arithmetic and copies ran while one was open for 4% -> 0% of each run, Pallas kernels for 0% -> 0%
where the time goes in v1:
time: 74.3 us; the launch traced here: 74.1 us
  Pallas kernels  71.3 us (96%)
  local copies, waits for them, and re-layouts  2.82 us (4%)
    pallas_call x1, Pallas kernels, on_device(): pl.pallas_call(functools.partial(square_kernel, sizes), out_shape=jax.Sha...  71.3 us
    unnamed x5, local copies, waits for them, and re-layouts  2.82 us

profile of v1, /device:TPU:1, one launch (start us, length us, event | category | flops | bytes accessed | tf_op | source)
XLA Modules:
  0.0 74.1 jit_solution(6270583815244595562)
XLA Ops:
  0.0 0.0 copy-start
  0.0 1.1 %copy-done = bf16[4,10,64,128]{3,2,1,0:T(8,128)(2,1)S(1)} copy-done((bf16[4,10,64,128]{3,2,1,0:T(8,128)(2,1)S(1)}, bf16[4,10,64,128]{3,2,1,0:T(8,128)(2,1)}, u32[]{:S(2)}) %copy-start) | copy-done | bytes 655384
  1.1 0.0 copy-start.1
  1.1 0.9 %copy-done.1 = s32[1536,10]{0,1:T(8,128)S(1)} copy-done((s32[1536,10]{0,1:T(8,128)S(1)}, s32[1536,10]{0,1:T(8,128)}, u32[]{:S(2)}) %copy-start.1) | copy-done | bytes 61464
  2.0 71.3 %square.1 = bf16[4,10,64,128]{3,2,1,0:T(8,128)(2,1)S(1)} custom-call(s32[10,1536]{1,0:T(8,128)S(1)} %bitcast.1, bf16[4,10,64,128]{3,2,1,0:T(8,128)(2,1)S(1)} %copy-done), custom_call_target="tpu_custom_call" | custom-call | tf_op jit(solution)/shard_map/square/pallas_call | solution.py:123
  73.3 0.8 %copy.4 = bf16[4,10,64,128]{3,2,1,0:T(8,128)(2,1)} copy(bf16[4,10,64,128]{3,2,1,0:T(8,128)(2,1)S(1)} %square.1) | data formatting | bytes 1310720
Async XLA Ops:
  0.0 1.1 %copy-start = (bf16[4,10,64,128]{3,2,1,0:T(8,128)(2,1)S(1)}, bf16[4,10,64,128]{3,2,1,0:T(8,128)(2,1)}, u32[]{:S(2)}) copy-start(bf16[4,10,64,128]{3,2,1,0:T(8,128)(2,1)} %values_ref.1) | copy-start | bytes 1966084
  1.1 0.9 %copy-start.1 = (s32[1536,10]{0,1:T(8,128)S(1)}, s32[1536,10]{0,1:T(8,128)}, u32[]{:S(2)}) copy-start(s32[1536,10]{0,1:T(8,128)} %param.3) | copy-start | bytes 184324

commit v2 on v1

--- a/solution.py
+++ b/solution.py
@@ -8,10 +8,16 @@
 from jax.sharding import PartitionSpec as P
 
 HOPS = 3
-
-
-def square_kernel(sizes, columns_ref, values_ref, out_ref, near, own, table, place,
-                  hop_send, hop_recv, core_send, core_recv, local_sem):
+REACH = 12
+SPAN = 2 * REACH
+STREAM = 48
+CHUNK = 8
+LEAD = 2 * CHUNK
+MESH = pl.DeviceIdType.MESH
+
+
+def whole_kernel(sizes, columns_ref, values_ref, out_ref, near, own, table, place,
+                 hop_send, hop_recv, core_send, core_recv, local_sem):
     rows_axis, cols_axis = sizes
     positions = rows_axis * cols_axis
     rows_here, slots, half, width = values_ref.shape
@@ -37,13 +43,13 @@
         return pltpu.make_async_remote_copy(
             source, unit_rows(HOPS - direction * (h + 1), r),
             hop_send.at[h, index, r], hop_recv.at[h, index, r],
-            device_id=at(direction), device_id_type=pl.DeviceIdType.MESH)
+            device_id=at(direction), device_id_type=MESH)
 
     def across(unit, r):
         source = values_ref.at[r] if unit == HOPS else unit_rows(unit, r)
         return pltpu.make_async_remote_copy(
             source, unit_rows(unit, r), core_send.at[unit, r], core_recv.at[unit, r],
-            device_id=sibling, device_id_type=pl.DeviceIdType.MESH)
+            device_id=sibling, device_id_type=MESH)
 
     table_copy = pltpu.make_async_copy(columns_ref, table, local_sem.at[0])
     own_copy = pltpu.make_async_copy(values_ref, own, local_sem.at[1])
@@ -52,7 +58,7 @@
 
     barrier = pltpu.get_barrier_semaphore()
     for peer in (at(1), at(-1), sibling):
-        pl.semaphore_signal(barrier, inc=1, device_id=peer, device_id_type=pl.DeviceIdType.MESH)
+        pl.semaphore_signal(barrier, inc=1, device_id=peer, device_id_type=MESH)
     pl.semaphore_wait(barrier, 3)
 
     for r in range(rows_here):
@@ -117,18 +123,18 @@
             across(unit, r).wait_send()
 
 
-def on_device(sizes, values, columns):
+def whole_square(sizes, table, values):
     rows_here, slots, half, width = values.shape
     units = 2 * HOPS + 1
     return pl.pallas_call(
-        functools.partial(square_kernel, sizes),
+        functools.partial(whole_kernel, sizes),
         out_shape=jax.ShapeDtypeStruct(values.shape, values.dtype),
-        in_specs=[pl.BlockSpec(memory_space=pltpu.HBM), pl.BlockSpec(memory_space=pltpu.HBM)],
+        in_specs=[pl.BlockSpec(memory_space=pl.ANY), pl.BlockSpec(memory_space=pl.ANY)],
         out_specs=pl.BlockSpec(memory_space=pltpu.VMEM),
         scratch_shapes=[
             pltpu.VMEM((units * rows_here * slots + 1, 2 * half, width), values.dtype),
             pltpu.VMEM(values.shape, values.dtype),
-            pltpu.SMEM(columns.shape[::-1], jnp.int32),
+            pltpu.SMEM(table.shape, jnp.int32),
             pltpu.SMEM((rows_here * slots * slots,), jnp.int32),
             pltpu.SemaphoreType.DMA((HOPS, 2, rows_here)),
             pltpu.SemaphoreType.DMA((HOPS, 2, rows_here)),
@@ -137,9 +143,367 @@
             pltpu.SemaphoreType.DMA((2 + rows_here,)),
         ],
         compiler_params=pltpu.CompilerParams(
-            collective_id=0, has_side_effects=True, vmem_limit_bytes=32 << 20),
-        name="square",
-    )(columns.T, values)
+            collective_id=1, has_side_effects=True, vmem_limit_bytes=56 << 20),
+        name="whole_square",
+    )(table, values)
+
+
+def shifted_mask(mask, step):
+    return mask << -step if step < 0 else mask >> step
+
+
+def stream_lengths(table_ref, total_rows, rows_here):
+    table = table_ref[...]
+    lane = lax.broadcasted_iota(jnp.int32, table.shape, 1)
+    place = table - lane + REACH
+    place = jnp.where(place < 0, place + total_rows, place)
+    place = jnp.where(place >= total_rows, place - total_rows, place)
+    place = jnp.clip(place, 0, SPAN)
+    masks = jnp.sum(jnp.left_shift(jnp.ones_like(place), place), axis=0, keepdims=True)
+    masks = jnp.broadcast_to(masks, (8, total_rows))
+    own_row = lax.broadcasted_iota(jnp.int32, masks.shape, 1) % rows_here
+
+    def ahead(array, steps):
+        return pltpu.roll(array, (-steps) % total_rows, 1)
+
+    longest = jnp.zeros((1, total_rows), jnp.int32)
+    for direction in (1, -1):
+        wanted = {}
+        for away in (2, 3):
+            got = jnp.zeros_like(masks)
+            for step in range(away * rows_here - rows_here + 1, away * rows_here + rows_here):
+                if step > REACH:
+                    continue
+                step = direction * step
+                there = ahead(masks, step)
+                row_there = own_row + step - direction * away * rows_here
+                use = (row_there >= 0) & (row_there < rows_here)
+                use = use & (((there >> (REACH - step)) & 1) == 1)
+                got = got | jnp.where(use, shifted_mask(there, -step), 0)
+            wanted[away] = got[0:1]
+
+        def count(mask):
+            hits = jnp.sum((jnp.broadcast_to(mask, place.shape) >> place) & 1, axis=0, keepdims=True)
+            hits = jnp.broadcast_to(hits, (8, total_rows))
+            summed = hits
+            for r in range(1, rows_here):
+                summed = summed + ahead(hits, r)
+            return summed
+
+        first = jnp.maximum(count(wanted[2] | wanted[3]), LEAD)
+        second = ahead(count(wanted[3]), -direction * rows_here)
+        longest = jnp.maximum(longest, jnp.where(own_row == 0, first + second, 0)[0:1])
+    return jnp.max(longest)
+
+
+def sparse_kernel(sizes, columns_ref, values_ref, out_ref, longest_ref, mine, theirs, landed, packed, left_side,
+                  table, table_rows, masks, needs, order, slot_of, place,
+                  unit_send, unit_recv, stream_send, stream_recv, core_send, core_recv, local_sem):
+    rows_axis, cols_axis = sizes
+    positions = rows_axis * cols_axis
+    blocks, half, width = values_ref.shape
+    rows_here, slots = out_ref.shape[:2]
+    total_rows = rows_here * positions
+    row, col, layer = lax.axis_index("row"), lax.axis_index("col"), lax.axis_index("layer")
+    position = row * cols_axis + col
+    first_row = position * rows_here
+    chunks = STREAM // CHUNK
+    directions = (1, -1)
+    unit_base = (blocks, 2 * blocks)
+    stream_base = (3 * blocks, 3 * blocks + STREAM)
+    empty = 3 * blocks + 2 * STREAM
+    units = 2 * HOPS + 1
+
+    def at(offset):
+        there = lax.rem(position + offset + positions, positions)
+        return (there // cols_axis, lax.rem(there, cols_axis), layer)
+
+    sibling = (row, col, 1 - layer)
+
+    def unit_copy(d, r):
+        part = pl.ds(unit_base[d] + r * slots, slots)
+        return pltpu.make_async_remote_copy(
+            values_ref.at[pl.ds(r * slots, slots)], mine.at[part], unit_send.at[d, r], unit_recv.at[d, r],
+            device_id=at(directions[d]), device_id_type=MESH)
+
+    def stream_copy(d, c):
+        part = pl.ds(c * CHUNK, CHUNK)
+        return pltpu.make_async_remote_copy(
+            packed.at[d, part], landed.at[d, part], stream_send.at[d, c], stream_recv.at[d, c],
+            device_id=at(directions[d]), device_id_type=MESH)
+
+    def own_across():
+        return pltpu.make_async_remote_copy(
+            values_ref, theirs.at[pl.ds(0, blocks)], core_send.at[0], core_recv.at[0],
+            device_id=sibling, device_id_type=MESH)
+
+    def unit_across(d, r):
+        part = pl.ds(unit_base[d] + r * slots, slots)
+        index = 1 + d * rows_here + r
+        return pltpu.make_async_remote_copy(
+            mine.at[part], theirs.at[part], core_send.at[index], core_recv.at[index],
+            device_id=sibling, device_id_type=MESH)
+
+    def stream_across(d, c):
+        index = 1 + 2 * rows_here + d * chunks + c
+        return pltpu.make_async_remote_copy(
+            landed.at[d, pl.ds(c * CHUNK, CHUNK)], theirs.at[pl.ds(stream_base[d] + c * CHUNK, CHUNK)],
+            core_send.at[index], core_recv.at[index], device_id=sibling, device_id_type=MESH)
+
+    table_copy = pltpu.make_async_copy(columns_ref, table, local_sem.at[0])
+    rows_copy = pltpu.make_async_copy(columns_ref, table_rows, local_sem.at[1])
+    own_copy = pltpu.make_async_copy(values_ref, mine.at[pl.ds(0, blocks)], local_sem.at[2])
+    table_copy.start()
+    rows_copy.start()
+    own_copy.start()
+
+    barrier = pltpu.get_barrier_semaphore()
+    for peer in (at(1), at(-1), sibling):
+        pl.semaphore_signal(barrier, inc=1, device_id=peer, device_id_type=MESH)
+    pl.semaphore_wait(barrier, 3)
+
+    for r in range(rows_here):
+        for d in range(2):
+            unit_copy(d, r).start()
+    own_across().start()
+    mine[empty] = jnp.zeros((half, width), mine.dtype)
+    theirs[empty] = jnp.zeros((half, width), mine.dtype)
+
+    table_copy.wait()
+
+    def wrapped(value):
+        value = jnp.where(value < 0, value + total_rows, value)
+        return jnp.where(value >= total_rows, value - total_rows, value)
+
+    def distance(entry, i):
+        return jnp.clip(wrapped(entry - i + REACH), 0, SPAN)
+
+    @pl.loop(0, 5 * rows_here)
+    def _(n):
+        i = wrapped(first_row - 2 * rows_here + n)
+        mask = jnp.int32(0)
+        for k in range(slots):
+            mask = mask | (jnp.int32(1) << distance(table[k, i], i))
+        masks[n] = mask
+
+    def need(source, receiver, r):
+        got = jnp.int32(0)
+        for t in range(rows_here):
+            step = rows_here * (source - receiver) + r - t
+            if abs(step) <= REACH:
+                mask = masks[rows_here * (receiver + 2) + t]
+                got = got | jnp.where(((mask >> (step + REACH)) & 1) == 1, shifted_mask(mask, step), 0)
+        return got
+
+    for d, sign in enumerate(directions):
+        pairs = ((-1, 1), (-1, 2), (-2, 0), (-2, 1), (-3, 0))
+        for n, (source, receiver) in enumerate(pairs):
+            for r in range(rows_here):
+                needs[(d * len(pairs) + n) * rows_here + r] = need(sign * source, sign * receiver, r)
+
+        def flag(n, r, e):
+            return (needs[(d * len(pairs) + n) * rows_here + r] >> e) & 1
+
+        def of_block(source, step):
+            r, s = step // slots, lax.rem(step, slots)
+            j = wrapped(first_row + sign * source * rows_here + r)
+            return r, distance(table[s, j], j)
+
+        word = blocks // 2
+
+        def gather(step, carry):
+            far_low, far_high, near_low, near_high, count = carry
+            r, e = of_block(-1, step)
+            far = flag(1, r, e)
+            close = flag(0, r, e) & (1 - far)
+            low = step < word
+            bit = jnp.where(low, step, step - word)
+            far_bit, near_bit = far << bit, close << bit
+            return (far_low | jnp.where(low, far_bit, 0), far_high | jnp.where(low, 0, far_bit),
+                    near_low | jnp.where(low, near_bit, 0), near_high | jnp.where(low, 0, near_bit),
+                    count + far + close)
+
+        zero = jnp.int32(0)
+        *words, count = lax.fori_loop(0, blocks, gather, (zero,) * 5)
+        lead = jnp.maximum(count, LEAD)
+
+        def arrange(s, carry):
+            lowest, found, done = [], zero, jnp.bool_(False)
+            rest = []
+            for n, bits in enumerate(carry):
+                take = jnp.logical_and(bits != 0, jnp.logical_not(done))
+                one = bits & -bits
+                index = zero
+                for level in range(5):
+                    pattern = sum(1 << b for b in range(word) if (b >> level) & 1)
+                    index = index + jnp.where((one & pattern) != 0, 1 << level, 0)
+                found = jnp.where(take, index + (n % 2) * word, found)
+                rest.append(jnp.where(take, bits ^ one, bits))
+                done = jnp.logical_or(done, take)
+            order[d * STREAM + s] = jnp.where(s < lead, unit_base[d] + found, stream_base[d] + s - lead)
+            return tuple(rest)
+
+        lax.fori_loop(0, STREAM, arrange, tuple(words))
+
+        def far_count(step, carry):
+            r, e = of_block(-2, step)
+            return carry + flag(3, r, e)
+
+        far_total = lax.fori_loop(0, blocks, far_count, zero)
+
+        def second(step, carry):
+            far_seen, near_seen = carry
+            r, e = of_block(-2, step)
+            far = flag(3, r, e)
+            close = flag(2, r, e) & (1 - far)
+            spot = jnp.where(far == 1, far_seen, far_total + near_seen)
+            slot_of[(HOPS - 2 * sign) * blocks + step] = stream_base[d] + jnp.minimum(spot, STREAM - 1)
+            return far_seen + far, near_seen + close
+
+        far_seen, near_seen = lax.fori_loop(0, blocks, second, (zero, zero))
+        start = jnp.maximum(far_seen + near_seen, LEAD)
+
+        def third(step, carry):
+            r, e = of_block(-3, step)
+            slot_of[(HOPS - 3 * sign) * blocks + step] = stream_base[d] + jnp.minimum(start + carry, STREAM - 1)
+            return carry + flag(4, r, e)
+
+        lax.fori_loop(0, blocks, third, zero)
+
+        @pl.loop(0, blocks)
+        def _(step):
+            slot_of[(HOPS - sign) * blocks + step] = unit_base[d] + step
+
+    @pl.loop(0, blocks)
+    def _(step):
+        slot_of[HOPS * blocks + step] = step
+
+    def find(step):
+        t, k = step // slots, lax.rem(step, slots)
+        i = first_row + t
+        j = table[k, i]
+        base = jnp.minimum(wrapped(j - first_row + HOPS * rows_here), units * rows_here - 1) * slots
+        there = [table[s, j] for s in range(slots)]
+        for m in range(slots):
+            wanted = table[m, i]
+            found = jnp.int32(-1)
+            for s in range(slots):
+                found = jnp.where(there[s] == wanted, s, found)
+            spot = slot_of[base + jnp.maximum(found, 0)]
+            place[step * slots + m] = jnp.where(found < 0, empty, spot)
+
+    own_copy.wait()
+    for t in range(rows_here):
+        for k in range(slots):
+            block = mine[t * slots + k]
+            turned = jnp.concatenate([block[:, width // 2:], block[:, :width // 2]], axis=1)
+            left_side[t, :, k * width:(k + 1) * width] = jnp.where(layer == 0, block, turned)
+
+    for r in range(rows_here):
+        for d in range(2):
+            unit_copy(d, r).wait_recv()
+            unit_across(d, r).start()
+
+    def take(d, c):
+        stream_copy(d, c).wait_recv()
+        stream_across(d, c).start()
+        mine[pl.ds(stream_base[d] + c * CHUNK, CHUNK)] = landed[d, pl.ds(c * CHUNK, CHUNK)]
+
+    for c in range(chunks):
+        for d in range(2):
+            if c * CHUNK >= LEAD:
+                take(d, c - LEAD // CHUNK)
+            for s in range(c * CHUNK, (c + 1) * CHUNK):
+                packed[d, s] = mine[order[d * STREAM + s]]
+            stream_copy(d, c).start()
+        if c < chunks - 1:
+            pl.loop(c * blocks // (chunks - 1), (c + 1) * blocks // (chunks - 1))(find)
+        if c == chunks - 1:
+            rows_copy.wait()
+            longest_ref[0, 0] = stream_lengths(table_rows, total_rows, rows_here)
+    for c in range(chunks - LEAD // CHUNK, chunks):
+        for d in range(2):
+            take(d, c)
+
+    own_across().wait_recv()
+    for d in range(2):
+        for r in range(rows_here):
+            unit_across(d, r).wait_recv()
+        for c in range(chunks):
+            stream_across(d, c).wait_recv()
+
+    pairs = slots // 2
+
+    @pl.loop(0, rows_here * pairs, unroll=5)
+    def _(step):
+        t, pair = step // pairs, lax.rem(step, pairs)
+        first = t * slots * slots + 2 * pair
+
+        def block(index):
+            return jnp.concatenate([mine[index], theirs[index]], axis=0)
+
+        right = jnp.concatenate([
+            jnp.concatenate([block(place[first + k * slots]), block(place[first + k * slots + 1])], axis=1)
+            for k in range(slots)], axis=0)
+        product = jnp.dot(left_side[t], right, preferred_element_type=jnp.float32).astype(out_ref.dtype)
+        out_ref[t, 2 * pair] = product[:, :width]
+        out_ref[t, 2 * pair + 1] = product[:, width:]
+
+    own_across().wait_send()
+    for d in range(2):
+        for r in range(rows_here):
+            unit_copy(d, r).wait_send()
+            unit_across(d, r).wait_send()
+        for c in range(chunks):
+            stream_copy(d, c).wait_send()
+            stream_across(d, c).wait_send()
+
+
+def sparse_square(sizes, table, values):
+    rows_here, slots, half, width = values.shape
+    blocks = rows_here * slots
+    spots = 3 * blocks + 2 * STREAM + 1
+    units = 2 * HOPS + 1
+    chunks = STREAM // CHUNK
+    crossings = 1 + 2 * rows_here + 2 * chunks
+    return pl.pallas_call(
+        functools.partial(sparse_kernel, sizes),
+        out_shape=[jax.ShapeDtypeStruct(values.shape, values.dtype), jax.ShapeDtypeStruct((1, 1), jnp.int32)],
+        in_specs=[pl.BlockSpec(memory_space=pl.ANY), pl.BlockSpec(memory_space=pl.ANY)],
+        out_specs=[pl.BlockSpec(memory_space=pltpu.VMEM), pl.BlockSpec(memory_space=pltpu.SMEM)],
+        scratch_shapes=[
+            pltpu.VMEM((spots, half, width), values.dtype),
+            pltpu.VMEM((spots, half, width), values.dtype),
+            pltpu.VMEM((2, STREAM, half, width), values.dtype),
+            pltpu.VMEM((2, STREAM, half, width), values.dtype),
+            pltpu.VMEM((rows_here, half, slots * width), values.dtype),
+            pltpu.SMEM(table.shape, jnp.int32),
+            pltpu.VMEM(table.shape, jnp.int32),
+            pltpu.SMEM((5 * rows_here,), jnp.int32),
+            pltpu.SMEM((10 * rows_here,), jnp.int32),
+            pltpu.SMEM((2 * STREAM,), jnp.int32),
+            pltpu.SMEM((units * blocks,), jnp.int32),
+            pltpu.SMEM((blocks * slots,), jnp.int32),
+            pltpu.SemaphoreType.DMA((2, rows_here)),
+            pltpu.SemaphoreType.DMA((2, rows_here)),
+            pltpu.SemaphoreType.DMA((2, chunks)),
+            pltpu.SemaphoreType.DMA((2, chunks)),
+            pltpu.SemaphoreType.DMA((crossings,)),
+            pltpu.SemaphoreType.DMA((crossings,)),
+            pltpu.SemaphoreType.DMA((3,)),
+        ],
+        compiler_params=pltpu.CompilerParams(
+            collective_id=0, has_side_effects=True, vmem_limit_bytes=56 << 20),
+        name="sparse_square",
+    )(table, values.reshape(blocks, half, width))
+
+
+def on_device(sizes, values, columns):
+    table = columns.T
+    square, longest = sparse_square(sizes, table, values)
+    return lax.cond(longest[0, 0] > STREAM,
+                    lambda: whole_square(sizes, table, values),
+                    lambda: square)
 
 
 def solution(mesh):

time: 74.3 us -> 68.1 us (0.917)
  Pallas kernels: 71.3 us -> 66.4 us
  local copies, waits for them, and re-layouts: 2.82 us -> 0.85 us
    pallas_call x1, Pallas kernels: 71.3 us -> 66.4 us  [sparse_square(): pl.pallas_call(functools.partial(sparse_kernel, sizes), out_shape=[jax.Sh...]
    unnamed x5, local copies, waits for them, and re-layouts: 2.82 us -> 0.85 us
where the time goes in v2:
time: 68.1 us; the launch traced here: 67.9 us
  Pallas kernels  66.4 us (98%)
  local copies, waits for them, and re-layouts  0.85 us (1%)
    pallas_call x1, Pallas kernels, sparse_square(): pl.pallas_call(functools.partial(sparse_kernel, sizes), out_shape=[jax.Sh...  66.4 us

profile of v2, /device:TPU:1, one launch (start us, length us, event | category | flops | bytes accessed | tf_op | source)
XLA Modules:
  0.0 67.9 jit_solution(16324769975545873198)
XLA Ops:
  0.0 0.0 copy-start
  0.0 0.0 copy-start.1
  0.0 66.4 %sparse_square.1 = (bf16[4,10,64,128]{3,2,1,0:T(8,128)(2,1)S(1)}, s32[1,1]{1,0:T(1,128)}) custom-call(s32[10,1536]{1,0:T(8,128)} %bitcast.4, bf16[40,64,128]{2,1,0:T(8,128)(2,1)} %bitcast.3), custom_call_target="tpu_custom_call" | custom-call | tf_op jit(solution)/shard_map/sparse_square/pallas_call | solution.py:469
  67.1 0.0 copy-done
  67.1 0.0 copy-done.1
  67.1 0.8 %copy.8 = bf16[4,10,64,128]{3,2,1,0:T(8,128)(2,1)} copy(bf16[4,10,64,128]{3,2,1,0:T(8,128)(2,1)S(1)} %get-tuple-element.19) | data formatting | bytes 1310720
  (1 shorter events, 0.0 us)
Async XLA Ops:
  0.0 67.1 %copy-start = (bf16[4,10,64,128]{3,2,1,0:T(8,128)(2,1)S(1)}, bf16[4,10,64,128]{3,2,1,0:T(8,128)(2,1)}, u32[]{:S(2)}) copy-start(bf16[4,10,64,128]{3,2,1,0:T(8,128)(2,1)} %param.4) | copy-start | bytes 1966084
  0.0 67.1 %copy-start.1 = (s32[1536,10]{0,1:T(8,128)S(1)}, s32[1536,10]{0,1:T(8,128)}, u32[]{:S(2)}) copy-start(s32[1536,10]{0,1:T(8,128)} %param.5) | copy-start | bytes 184324

commit v3 on v2

v3 whole, which is shorter than its diff:
```python
import functools

import jax
import jax.numpy as jnp
from jax import lax
from jax.experimental import pallas as pl
from jax.experimental.pallas import tpu as pltpu
from jax.sharding import PartitionSpec as P

HOPS = 3
REACH = 12
SPAN = 2 * REACH
STREAM = 92
SEAM_STREAM = 84
CHUNK = 4
LAG = 5
FIRST_LAG = 3
MESH = pl.DeviceIdType.MESH


def whole_kernel(sizes, columns_ref, values_ref, out_ref, near, own, table, place,
                 hop_send, hop_recv, core_send, core_recv, local_sem):
    rows_axis, cols_axis = sizes
    positions = rows_axis * cols_axis
    rows_here, slots, half, width = values_ref.shape
    total_rows = rows_here * positions
    row, col, layer = lax.axis_index("row"), lax.axis_index("col"), lax.axis_index("layer")
    position = row * cols_axis + col
    units = 2 * HOPS + 1
    empty = units * rows_here * slots

    def at(offset):
        there = lax.rem(position + offset + positions, positions)
        return (there // cols_axis, lax.rem(there, cols_axis), layer)

    sibling = (row, col, 1 - layer)
    my_half = pl.ds(pl.multiple_of(layer * half, half), half)

    def unit_rows(unit, r):
        return near.at[pl.ds((unit * rows_here + r) * slots, slots), my_half, :]

    def hop(h, direction, r):
        index = 0 if direction > 0 else 1
        source = values_ref.at[r] if h == 0 else unit_rows(HOPS - direction * h, r)
        return pltpu.make_async_remote_copy(
            source, unit_rows(HOPS - direction * (h + 1), r),
            hop_send.at[h, index, r], hop_recv.at[h, index, r],
            device_id=at(direction), device_id_type=MESH)

    def across(unit, r):
        source = values_ref.at[r] if unit == HOPS else unit_rows(unit, r)
        return pltpu.make_async_remote_copy(
            source, unit_rows(unit, r), core_send.at[unit, r], core_recv.at[unit, r],
            device_id=sibling, device_id_type=MESH)

    table_copy = pltpu.make_async_copy(columns_ref, table, local_sem.at[0])
    own_copy = pltpu.make_async_copy(values_ref, own, local_sem.at[1])
    table_copy.start()
    own_copy.start()

    barrier = pltpu.get_barrier_semaphore()
    for peer in (at(1), at(-1), sibling):
        pl.semaphore_signal(barrier, inc=1, device_id=peer, device_id_type=MESH)
    pl.semaphore_wait(barrier, 3)

    for r in range(rows_here):
        for direction in (1, -1):
            hop(0, direction, r).start()
    for r in range(rows_here):
        across(HOPS, r).start()
    near[empty] = jnp.zeros((2 * half, width), near.dtype)
    near_own = [pltpu.make_async_copy(values_ref.at[r], unit_rows(HOPS, r), local_sem.at[2 + r]) for r in range(rows_here)]
    for copy in near_own:
        copy.start()
    table_copy.wait()

    @pl.loop(0, rows_here * slots)
    def _(step):
        t, k = step // slots, lax.rem(step, slots)
        i = position * rows_here + t
        j = table[k, i]
        base = lax.rem(j - position * rows_here + HOPS * rows_here + total_rows, total_rows) * slots
        there = [table[s, j] for s in range(slots)]
        for m in range(slots):
            wanted = table[m, i]
            found = empty
            for s in range(slots):
                found = jnp.where(there[s] == wanted, base + s, found)
            place[step * slots + m] = jnp.minimum(found, empty)

    for h in range(HOPS):
        for r in range(rows_here):
            for direction in (1, -1):
                hop(h, direction, r).wait_recv()
                if h + 1 < HOPS:
                    hop(h + 1, direction, r).start()
                across(HOPS - direction * (h + 1), r).start()
    own_copy.wait()
    for copy in near_own:
        copy.wait()
    for unit in range(units):
        for r in range(rows_here):
            across(unit, r).wait_recv()

    pairs = slots // 2

    @pl.loop(0, rows_here * pairs)
    def _(step):
        t, pair = step // pairs, lax.rem(step, pairs)
        left = jnp.concatenate([own[t, k] for k in range(slots)], axis=1)
        first = t * slots * slots + 2 * pair
        right = jnp.concatenate([
            jnp.concatenate([near[place[first + k * slots]], near[place[first + k * slots + 1]]], axis=1)
            for k in range(slots)], axis=0)
        product = jnp.dot(left, right, preferred_element_type=jnp.float32).astype(out_ref.dtype)
        out_ref[t, 2 * pair] = product[:, :width]
        out_ref[t, 2 * pair + 1] = product[:, width:]

    for h in range(HOPS):
        for r in range(rows_here):
            for direction in (1, -1):
                hop(h, direction, r).wait_send()
    for unit in range(units):
        for r in range(rows_here):
            across(unit, r).wait_send()


def whole_square(sizes, table, values):
    rows_here, slots, half, width = values.shape
    units = 2 * HOPS + 1
    return pl.pallas_call(
        functools.partial(whole_kernel, sizes),
        out_shape=jax.ShapeDtypeStruct(values.shape, values.dtype),
        in_specs=[pl.BlockSpec(memory_space=pl.ANY), pl.BlockSpec(memory_space=pl.ANY)],
        out_specs=pl.BlockSpec(memory_space=pltpu.VMEM),
        scratch_shapes=[
            pltpu.VMEM((units * rows_here * slots + 1, 2 * half, width), values.dtype),
            pltpu.VMEM(values.shape, values.dtype),
            pltpu.SMEM(table.shape, jnp.int32),
            pltpu.SMEM((rows_here * slots * slots,), jnp.int32),
            pltpu.SemaphoreType.DMA((HOPS, 2, rows_here)),
            pltpu.SemaphoreType.DMA((HOPS, 2, rows_here)),
            pltpu.SemaphoreType.DMA((units, rows_here)),
            pltpu.SemaphoreType.DMA((units, rows_here)),
            pltpu.SemaphoreType.DMA((2 + rows_here,)),
        ],
        compiler_params=pltpu.CompilerParams(
            collective_id=1, has_side_effects=True, vmem_limit_bytes=56 << 20),
        name="whole_square",
    )(table, values)


def shifted_mask(mask, step):
    return mask << -step if step < 0 else mask >> step


def seam_streams(col, cols_axis):
    return (col >= cols_axis - 1) | (col <= 1)


def layout(first, tail, far_first, far_tail, last_first, last_tail, behind, larger):
    lead = LAG * CHUNK

    def starts(n):
        one = larger(first + behind(tail, n), first + FIRST_LAG * CHUNK)
        two = larger(one + behind(far_first, n + 1),
                     first + behind(tail, n + 1) - behind(last_tail, n + 1) + lead)
        return one, two

    one, two = starts(0)
    one_behind, two_behind = starts(1)
    three = larger(two + behind(far_tail, 1), one_behind + lead)
    four = larger(three + behind(last_first, 2), two_behind + lead)
    return one, two, three, four, four + behind(last_tail, 2)


def stream_excess(table_ref, total_rows, rows_here, cols_axis):
    table = table_ref[...]
    slots = table.shape[0]
    lane = lax.broadcasted_iota(jnp.int32, table.shape, 1)
    place = (table - lane + REACH) & 31
    masks = jnp.sum(jnp.left_shift(jnp.ones_like(place), place), axis=0, keepdims=True)
    masks = jnp.broadcast_to(masks, (8, total_rows))
    own_row_index = lax.broadcasted_iota(jnp.int32, masks.shape, 1)
    own_row = own_row_index % rows_here

    def ahead(array, steps):
        return pltpu.roll(array, (-steps) % total_rows, 1)

    seam = seam_streams((own_row_index // rows_here) % cols_axis, cols_axis)
    most = jnp.full((1, total_rows), -STREAM, jnp.int32)
    for direction in (1, -1):
        wanted = {}
        for away in range(1, HOPS + 1):
            got = jnp.zeros_like(masks)
            for step in range(away * rows_here - rows_here + 1, away * rows_here + rows_here):
                if step > REACH:
                    continue
                step = direction * step
                there = ahead(masks, step)
                row_there = own_row + step - direction * away * rows_here
                use = (row_there >= 0) & (row_there < rows_here)
                use = use & (((there >> (REACH - step)) & 1) == 1)
                got = got | jnp.where(use, shifted_mask(there, -step), 0)
            wanted[away] = got[0:1]
        own_first = (own_row >= rows_here // 2) if direction > 0 else (own_row < rows_here // 2)

        def counts(mask):
            hits = jnp.sum((jnp.broadcast_to(mask, place.shape) >> place) & 1, axis=0, keepdims=True)
            hits = jnp.broadcast_to(hits, (8, total_rows))
            totals = []
            for part in (jnp.where(own_first, hits, 0), jnp.where(own_first, 0, hits)):
                summed = part
                for r in range(1, rows_here):
                    summed = summed + ahead(part, r)
                totals.append(summed)
            return totals

        _, tail = counts(wanted[1] | wanted[2] | wanted[3])
        far_first, far_tail = counts(wanted[2] | wanted[3])
        last_first, last_tail = counts(wanted[3])
        end = layout(rows_here // 2 * slots, tail, far_first, far_tail, last_first, last_tail,
                     lambda count, n: ahead(count, -direction * rows_here * n), jnp.maximum)[-1]
        room = jnp.where(seam, SEAM_STREAM, STREAM) if direction > 0 else STREAM
        most = jnp.maximum(most, jnp.where(own_row == 0, end - room, -STREAM)[0:1])
    return jnp.max(most)


def ones(bits):
    bits = bits - ((bits >> 1) & 0x55555555)
    bits = (bits & 0x33333333) + ((bits >> 2) & 0x33333333)
    bits = (bits + (bits >> 4)) & 0x0F0F0F0F
    return (bits * 0x01010101) >> 24


def lowest(bits, limit):
    one = bits & -bits
    index = jnp.int32(0)
    for level in range(5):
        pattern = sum(1 << b for b in range(limit) if (b >> level) & 1)
        index = index + jnp.where((one & pattern) != 0, 1 << level, 0)
    return index, bits ^ one


def sparse_kernel(sizes, columns_ref, values_ref, out_ref, excess_ref, own, mine, theirs, landed, packed, left_side,
                  table, table_rows, masks, needs, order, slot_of, place,
                  unit_send, unit_recv, stream_send, stream_recv, core_send, core_recv, local_sem):
    rows_axis, cols_axis = sizes
    positions = rows_axis * cols_axis
    blocks, half, width = values_ref.shape
    rows_here, slots = out_ref.shape[:2]
    total_rows = rows_here * positions
    row, col, layer = lax.axis_index("row"), lax.axis_index("col"), lax.axis_index("layer")
    position = row * cols_axis + col
    first_row = position * rows_here
    first_rows = rows_here // 2
    first = first_rows * slots
    chunks = (STREAM - first) // CHUNK
    directions = (1, -1)
    stream_base = (blocks, blocks + STREAM)
    empty = blocks + 2 * STREAM
    units = 2 * HOPS + 1

    def at(offset):
        there = lax.rem(position + offset + positions, positions)
        return (there // cols_axis, lax.rem(there, cols_axis), layer)

    sibling = (row, col, 1 - layer)

    def row_of(d, n):
        return rows_here - 1 - n if d == 0 else n

    def unit_copy(d, n):
        return pltpu.make_async_remote_copy(
            values_ref.at[pl.ds(row_of(d, n) * slots, slots)], mine.at[pl.ds(stream_base[d] + n * slots, slots)],
            unit_send.at[d, n], unit_recv.at[d, n], device_id=at(directions[d]), device_id_type=MESH)

    def stream_copy(d, c):
        part = pl.ds(c * CHUNK, CHUNK)
        return pltpu.make_async_remote_copy(
            packed.at[d, part], landed.at[d, part], stream_send.at[d, c], stream_recv.at[d, c],
            device_id=at(directions[d]), device_id_type=MESH)

    def own_across():
        return pltpu.make_async_remote_copy(
            values_ref, theirs.at[pl.ds(0, blocks)], core_send.at[0], core_recv.at[0],
            device_id=sibling, device_id_type=MESH)

    def unit_across(d, n):
        part = pl.ds(stream_base[d] + n * slots, slots)
        index = 1 + d * first_rows + n
        return pltpu.make_async_remote_copy(
            mine.at[part], theirs.at[part], core_send.at[index], core_recv.at[index],
            device_id=sibling, device_id_type=MESH)

    def stream_across(d, c):
        index = 1 + 2 * first_rows + d * chunks + c
        return pltpu.make_async_remote_copy(
            landed.at[d, pl.ds(c * CHUNK, CHUNK)], theirs.at[pl.ds(stream_base[d] + first + c * CHUNK, CHUNK)],
            core_send.at[index], core_recv.at[index], device_id=sibling, device_id_type=MESH)

    table_copy = pltpu.make_async_copy(columns_ref, table, local_sem.at[0])
    rows_copy = pltpu.make_async_copy(columns_ref, table_rows, local_sem.at[1])
    own_copy = pltpu.make_async_copy(values_ref, own, local_sem.at[2])
    mine_copy = pltpu.make_async_copy(values_ref, mine.at[pl.ds(0, blocks)], local_sem.at[3])
    table_copy.start()
    rows_copy.start()
    own_copy.start()
    mine_copy.start()

    barrier = pltpu.get_barrier_semaphore()
    for peer in (at(1), at(-1), sibling):
        pl.semaphore_signal(barrier, inc=1, device_id=peer, device_id_type=MESH)
    pl.semaphore_wait(barrier, 3)

    for n in range(first_rows):
        for d in range(2):
            unit_copy(d, n).start()
    own_across().start()
    mine[empty] = jnp.zeros((half, width), mine.dtype)
    theirs[empty] = jnp.zeros((half, width), mine.dtype)

    table_copy.wait()
    zero = jnp.int32(0)

    def wrapped(value):
        value = jnp.where(value < 0, value + total_rows, value)
        return jnp.where(value >= total_rows, value - total_rows, value)

    def distance(entry, i):
        return (entry - i + REACH) & 31

    @pl.loop(0, units * rows_here)
    def _(n):
        i = wrapped(first_row - HOPS * rows_here + n)
        mask = zero
        for k in range(slots):
            mask = mask | (jnp.int32(1) << distance(table[k, i], i))
        masks[n] = mask

    def unit_mask(unit, r):
        return masks[rows_here * (unit + HOPS) + r]

    def need(source, receiver, r):
        got = zero
        for t in range(rows_here):
            step = rows_here * (source - receiver) + r - t
            if abs(step) <= REACH:
                mask = unit_mask(receiver, t)
                got = got | jnp.where(((mask >> (step + REACH)) & 1) == 1, shifted_mask(mask, step), 0)
        return got

    def needs_at(d, back, n, which):
        return ((d * (HOPS + 1) + back) * rows_here + n) * 3 + which

    def fill_needs(d, back):
        sign = directions[d]
        for n in range(rows_here):
            r = row_of(d, n)
            near, far, last = (need(-sign * back, sign * (away - back), r) for away in (1, 2, 3))
            for which, bits in enumerate((near | far | last, far | last, last)):
                needs[needs_at(d, back, n, which)] = bits

    def of_row(d, back, n):
        r = row_of(d, n)
        j = wrapped(first_row - directions[d] * back * rows_here + r)
        wanted = [needs[needs_at(d, back, n, which)] for which in range(3)]
        blocks_here = []
        for s in range(slots):
            e = distance(table[s, j], j)
            blocks_here.append((r * slots + s, *((bits >> e) & 1 for bits in wanted)))
        return blocks_here

    def count(d, back, which, rows):
        total = zero
        for n in rows:
            bits = needs[needs_at(d, back, n, which)] & unit_mask(-directions[d] * back, row_of(d, n))
            total = total + ones(bits)
        return total

    firsts, tails = range(first_rows), range(first_rows, rows_here)

    for d in range(2):
        fill_needs(d, 0)

        bits = zero
        for n in tails:
            for s, (_, near, _, _) in enumerate(of_row(d, 0, n)):
                bits = bits | (near << ((n - first_rows) * slots + s))

        def natural(found):
            n = found // slots if d == 1 else 1 - found // slots
            base = first if d == 1 else 0
            return base + n * slots + lax.rem(found, slots)

        def arrange(s, bits):
            found, bits = lowest(bits, blocks - first)
            order[d * STREAM + s] = natural(found)
            return bits

        lax.fori_loop(first, blocks, arrange, bits)

    own_copy.wait()

    sends_short = seam_streams(col, cols_axis)
    gets_short = seam_streams(lax.rem(col + cols_axis - 1, cols_axis), cols_axis)

    def unless(short, d, c, step):
        if d == 0 and first + c * CHUNK >= SEAM_STREAM:
            pl.when(jnp.logical_not(short))(step)
        else:
            step()

    def pack(d, c, source):
        def step():
            for s in range(c * CHUNK, (c + 1) * CHUNK):
                packed[d, s] = source[order[d * STREAM + first + s]]
            stream_copy(d, c).start()
        unless(sends_short, d, c, step)

    for c in range(FIRST_LAG):
        for d in range(2):
            pack(d, c, own)

    for d, sign in enumerate(directions):
        for back in range(1, HOPS + 1):
            fill_needs(d, back)
        tail = [count(d, back, 0, tails) for back in range(HOPS + 1)]
        far_first, far_tail = ([count(d, back, 1, rows) for back in range(HOPS + 1)] for rows in (firsts, tails))
        last_first, last_tail = ([count(d, back, 2, rows) for back in range(HOPS + 1)] for rows in (firsts, tails))

        def starts(here):
            return layout(first, tail, far_first, far_tail, last_first, last_tail,
                          lambda counts, n: counts[min(here + n, HOPS)], jnp.maximum)

        one, two, three, four, _ = starts(0)
        one_in, two_in, three_in, four_in, _ = starts(1)
        base = stream_base[d]

        def note(back, block, spot):
            slot_of[(HOPS - sign * back) * blocks + block] = base + jnp.clip(spot, 0, STREAM - 1)

        words = []
        seen = zero
        for rows in (firsts, tails):
            last_bits = far_bits = zero
            for n in rows:
                for s, (block, near, far, last) in enumerate(of_row(d, 1, n)):
                    step = (n - rows[0]) * slots + s
                    last_bits = last_bits | (last << step)
                    far_bits = far_bits | ((far & (1 - last)) << step)
                    if rows is firsts:
                        note(1, block, step)
                    else:
                        note(1, block, first + seen)
                        seen = seen + near
            words += [last_bits, far_bits]

        for rows, start, total, later in ((firsts, one_in, last_first[2], three_in), (tails, two_in, last_tail[2], four_in)):
            last_spot, far_spot, spot = start, start + total, later
            for n in rows:
                for block, _, far, last in of_row(d, 2, n):
                    note(2, block, jnp.where(last == 1, last_spot, far_spot))
                    last_spot = last_spot + last
                    far_spot = far_spot + (far & (1 - last))
                for block, _, _, last in of_row(d, 3, n):
                    note(3, block, spot)
                    spot = spot + last

        def arrange(with_own, s, carry):
            bits_one, bits_two, bits_three, bits_four = carry
            from_first = s < two
            use_last = jnp.where(from_first, bits_one, bits_three) != 0
            bits = jnp.where(from_first, jnp.where(use_last, bits_one, bits_two),
                             jnp.where(use_last, bits_three, bits_four))
            found, rest = lowest(bits, first)
            n, r = found // slots, lax.rem(found, slots)
            n = jnp.where(from_first, n, first_rows + n)
            spot = slot_of[(HOPS - sign) * blocks + (rows_here - 1 - n if d == 0 else n) * slots + r]
            spot = jnp.where(s >= three, base + one_in + s - three, spot)
            spot = jnp.where(s >= four, base + two_in + s - four, spot)
            spot = jnp.clip(spot, 0, empty)
            active = True
            if with_own:
                active = s >= one
                spot = jnp.where(active, spot, order[d * STREAM + s])
            order[d * STREAM + s] = spot
            pick = [from_first & use_last, from_first & ~use_last, ~from_first & use_last, ~from_first & ~use_last]
            return tuple(jnp.where(p & active, rest, b) for p, b in zip(pick, carry))

        carry = lax.fori_loop(first + FIRST_LAG * CHUNK, blocks, functools.partial(arrange, True), tuple(words))
        lax.fori_loop(blocks, STREAM, functools.partial(arrange, False), carry)

    @pl.loop(0, blocks)
    def _(step):
        slot_of[HOPS * blocks + step] = step

    def find(step):
        t, k = step // slots, lax.rem(step, slots)
        i = first_row + t
        j = table[k, i]
        base = jnp.minimum(wrapped(j - first_row + HOPS * rows_here), units * rows_here - 1) * slots
        there = [table[s, j] for s in range(slots)]
        for m in range(slots):
            wanted = table[m, i]
            found = jnp.int32(-1)
            for s in range(slots):
                found = jnp.where(there[s] == wanted, s, found)
            spot = slot_of[base + jnp.maximum(found, 0)]
            place[step * slots + m] = jnp.where(found < 0, empty, spot)

    def take(d, c):
        def step():
            stream_copy(d, c).wait_recv()
            stream_across(d, c).start()
            mine[pl.ds(stream_base[d] + first + c * CHUNK, CHUNK)] = landed[d, pl.ds(c * CHUNK, CHUNK)]
        unless(gets_short, d, c, step)

    mine_copy.wait()
    for n in range(first_rows):
        for d in range(2):
            unit_copy(d, n).wait_recv()
            unit_across(d, n).start()

    shares = 10
    for c in range(FIRST_LAG, chunks):
        for d in range(2):
            if c >= LAG:
                take(d, c - LAG)
            pack(d, c, mine)
        n = c - FIRST_LAG
        if n < shares:
            pl.loop(n * blocks // shares, (n + 1) * blocks // shares)(find)
    rows_copy.wait()
    excess_ref[0, 0] = stream_excess(table_rows, total_rows, rows_here, cols_axis)
    for t in range(rows_here):
        for k in range(slots):
            block = own[t * slots + k]
            turned = jnp.concatenate([block[:, width // 2:], block[:, :width // 2]], axis=1)
            left_side[t, :, k * width:(k + 1) * width] = jnp.where(layer == 0, block, turned)
    for c in range(chunks - LAG, chunks):
        for d in range(2):
            take(d, c)

    own_across().wait_recv()
    for d in range(2):
        for n in range(first_rows):
            unit_across(d, n).wait_recv()
        for c in range(chunks):
            unless(gets_short, d, c, lambda d=d, c=c: stream_across(d, c).wait_recv())

    pairs = slots // 2

    @pl.loop(0, rows_here * pairs, unroll=5)
    def _(step):
        t, pair = step // pairs, lax.rem(step, pairs)
        start = t * slots * slots + 2 * pair

        def block(index):
            return jnp.concatenate([mine[index], theirs[index]], axis=0)

        right = jnp.concatenate([
            jnp.concatenate([block(place[start + k * slots]), block(place[start + k * slots + 1])], axis=1)
            for k in range(slots)], axis=0)
        product = jnp.dot(left_side[t], right, preferred_element_type=jnp.float32).astype(out_ref.dtype)
        out_ref[t, 2 * pair] = product[:, :width]
        out_ref[t, 2 * pair + 1] = product[:, width:]

    own_across().wait_send()
    for d in range(2):
        for n in range(first_rows):
            unit_copy(d, n).wait_send()
            unit_across(d, n).wait_send()
        for c in range(chunks):
            unless(sends_short, d, c, lambda d=d, c=c: stream_copy(d, c).wait_send())
            unless(gets_short, d, c, lambda d=d, c=c: stream_across(d, c).wait_send())


def sparse_square(sizes, table, values):
    rows_here, slots, half, width = values.shape
    blocks = rows_here * slots
    first_rows = rows_here // 2
    spots = blocks + 2 * STREAM + 1
    units = 2 * HOPS + 1
    chunks = (STREAM - first_rows * slots) // CHUNK
    crossings = 1 + 2 * first_rows + 2 * chunks
    return pl.pallas_call(
        functools.partial(sparse_kernel, sizes),
        out_shape=[jax.ShapeDtypeStruct(values.shape, values.dtype), jax.ShapeDtypeStruct((1, 1), jnp.int32)],
        in_specs=[pl.BlockSpec(memory_space=pl.ANY), pl.BlockSpec(memory_space=pl.ANY)],
        out_specs=[pl.BlockSpec(memory_space=pltpu.VMEM), pl.BlockSpec(memory_space=pltpu.SMEM)],
        scratch_shapes=[
            pltpu.VMEM((blocks, half, width), values.dtype),
            pltpu.VMEM((spots, half, width), values.dtype),
            pltpu.VMEM((spots, half, width), values.dtype),
            pltpu.VMEM((2, chunks * CHUNK, half, width), values.dtype),
            pltpu.VMEM((2, chunks * CHUNK, half, width), values.dtype),
            pltpu.VMEM((rows_here, half, slots * width), values.dtype),
            pltpu.SMEM(table.shape, jnp.int32),
            pltpu.VMEM(table.shape, jnp.int32),
            pltpu.SMEM((units * rows_here,), jnp.int32),
            pltpu.SMEM((2 * (HOPS + 1) * rows_here * 3,), jnp.int32),
            pltpu.SMEM((2 * STREAM,), jnp.int32),
            pltpu.SMEM((units * blocks,), jnp.int32),
            pltpu.SMEM((blocks * slots,), jnp.int32),
            pltpu.SemaphoreType.DMA((2, first_rows)),
            pltpu.SemaphoreType.DMA((2, first_rows)),
            pltpu.SemaphoreType.DMA((2, chunks)),
            pltpu.SemaphoreType.DMA((2, chunks)),
            pltpu.SemaphoreType.DMA((crossings,)),
            pltpu.SemaphoreType.DMA((crossings,)),
            pltpu.SemaphoreType.DMA((4,)),
        ],
        compiler_params=pltpu.CompilerParams(
            collective_id=0, has_side_effects=True, vmem_limit_bytes=56 << 20),
        name="sparse_square",
    )(table, values.reshape(blocks, half, width))


def on_device(sizes, values, columns):
    table = columns.T
    square, excess = sparse_square(sizes, table, values)
    return lax.cond(excess[0, 0] > 0,
                    lambda: whole_square(sizes, table, values),
                    lambda: square)


def solution(mesh):
    return jax.shard_map(
        functools.partial(on_device, (mesh.shape["row"], mesh.shape["col"])),
        mesh=mesh,
        in_specs=(P(("row", "col"), None, "layer", None), P()),
        out_specs=P(("row", "col"), None, "layer", None),
        check_vma=False,
    )
```

time: 68.1 us -> 61.1 us (0.90)
  Pallas kernels: 66.4 us -> 59.5 us
    pallas_call x1, Pallas kernels: 66.4 us -> 59.5 us  [sparse_square(): pl.pallas_call(functools.partial(sparse_kernel, sizes), out_shape=[jax.Sh...]
where the time goes in v3:
time: 61.1 us; the launch traced here: 61 us
  Pallas kernels  59.5 us (97%)
  local copies, waits for them, and re-layouts  0.85 us (1%)
  between operations  0.65 us (1%)
    pallas_call x1, Pallas kernels, sparse_square(): pl.pallas_call(functools.partial(sparse_kernel, sizes), out_shape=[jax.Sh...  59.5 us

profile of v3, /device:TPU:1, one launch (start us, length us, event | category | flops | bytes accessed | tf_op | source)
XLA Modules:
  0.0 61.0 jit_solution(3770555245629415914)
XLA Ops:
  0.0 0.0 copy-start
  0.0 0.0 copy-start.1
  0.0 59.5 %sparse_square.1 = (bf16[4,10,64,128]{3,2,1,0:T(8,128)(2,1)S(1)}, s32[1,1]{1,0:T(1,128)}) custom-call(s32[10,1536]{1,0:T(8,128)} %bitcast.4, bf16[40,64,128]{2,1,0:T(8,128)(2,1)} %bitcast.3), custom_call_target="tpu_custom_call" | custom-call | tf_op jit(solution)/shard_map/sparse_square/pallas_call | solution.py:587
  60.1 0.0 copy-done
  60.1 0.0 copy-done.1
  60.1 0.8 %copy.8 = bf16[4,10,64,128]{3,2,1,0:T(8,128)(2,1)} copy(bf16[4,10,64,128]{3,2,1,0:T(8,128)(2,1)S(1)} %get-tuple-element.19) | data formatting | bytes 1310720
  (1 shorter events, 0.0 us)
Async XLA Ops:
  0.0 60.1 %copy-start = (bf16[4,10,64,128]{3,2,1,0:T(8,128)(2,1)S(1)}, bf16[4,10,64,128]{3,2,1,0:T(8,128)(2,1)}, u32[]{:S(2)}) copy-start(bf16[4,10,64,128]{3,2,1,0:T(8,128)(2,1)} %param.4) | copy-start | bytes 1966084
  0.0 60.1 %copy-start.1 = (s32[1536,10]{0,1:T(8,128)S(1)}, s32[1536,10]{0,1:T(8,128)}, u32[]{:S(2)}) copy-start(s32[1536,10]{0,1:T(8,128)} %param.5) | copy-start | bytes 184324

commit v4 on v3

--- a/solution.py
+++ b/solution.py
@@ -11,10 +11,10 @@
 REACH = 12
 SPAN = 2 * REACH
 STREAM = 92
-SEAM_STREAM = 84
-CHUNK = 4
-LAG = 5
-FIRST_LAG = 3
+SEAM_STREAM = 78
+CHUNK = 2
+LAG = 7
+FIRST_LAG = 6
 MESH = pl.DeviceIdType.MESH
 
 
@@ -242,7 +242,7 @@
     return index, bits ^ one
 
 
-def sparse_kernel(sizes, columns_ref, values_ref, out_ref, excess_ref, own, mine, theirs, landed, packed, left_side,
+def sparse_kernel(sizes, columns_ref, values_ref, out_ref, excess_ref, rows_own, own, mine, every, landed, packed,
                   table, table_rows, masks, needs, order, slot_of, place,
                   unit_send, unit_recv, stream_send, stream_recv, core_send, core_recv, local_sem):
     rows_axis, cols_axis = sizes
@@ -256,69 +256,75 @@
     first_rows = rows_here // 2
     first = first_rows * slots
     chunks = (STREAM - first) // CHUNK
-    directions = (1, -1)
-    stream_base = (blocks, blocks + STREAM)
+    units = 2 * HOPS + 1
     empty = blocks + 2 * STREAM
-    units = 2 * HOPS + 1
+    own_frame, other_frame = layer, 1 - layer
 
     def at(offset):
         there = lax.rem(position + offset + positions, positions)
         return (there // cols_axis, lax.rem(there, cols_axis), layer)
 
+    ahead, behind = at(1 - 2 * layer), at(2 * layer - 1)
     sibling = (row, col, 1 - layer)
-
-    def row_of(d, n):
-        return rows_here - 1 - n if d == 0 else n
-
-    def unit_copy(d, n):
+    halves = [pl.ds(pl.multiple_of(which * half, half), half) for which in (layer, 1 - layer)]
+
+    def row_of(frame, r):
+        return jnp.where(frame == 0, r, rows_here - 1 - r)
+
+    def blocks_of(frame, r):
+        return pl.ds(row_of(frame, r) * slots, slots)
+
+    def stream_base(frame):
+        return blocks + frame * STREAM
+
+    def unit_copy(n, which):
+        r = rows_here - 1 - n
+        source = values_ref.at[blocks_of(own_frame, r)] if which == 0 else own.at[blocks_of(own_frame, r), halves[1], :]
         return pltpu.make_async_remote_copy(
-            values_ref.at[pl.ds(row_of(d, n) * slots, slots)], mine.at[pl.ds(stream_base[d] + n * slots, slots)],
-            unit_send.at[d, n], unit_recv.at[d, n], device_id=at(directions[d]), device_id_type=MESH)
-
-    def stream_copy(d, c):
+            source, mine.at[pl.ds(blocks + n * slots, slots), halves[which], :],
+            unit_send.at[n, which], unit_recv.at[n, which], device_id=ahead, device_id_type=MESH)
+
+    def stream_copy(c):
         part = pl.ds(c * CHUNK, CHUNK)
         return pltpu.make_async_remote_copy(
-            packed.at[d, part], landed.at[d, part], stream_send.at[d, c], stream_recv.at[d, c],
-            device_id=at(directions[d]), device_id_type=MESH)
-
-    def own_across():
+            packed.at[part], landed.at[part], stream_send.at[c], stream_recv.at[c],
+            device_id=ahead, device_id_type=MESH)
+
+    def own_across(r):
+        part = blocks_of(other_frame, r)
         return pltpu.make_async_remote_copy(
-            values_ref, theirs.at[pl.ds(0, blocks)], core_send.at[0], core_recv.at[0],
+            values_ref.at[part], own.at[part, halves[0], :], core_send.at[r], core_recv.at[r],
             device_id=sibling, device_id_type=MESH)
 
-    def unit_across(d, n):
-        part = pl.ds(stream_base[d] + n * slots, slots)
-        index = 1 + d * first_rows + n
+    def unit_across():
+        index = rows_here
         return pltpu.make_async_remote_copy(
-            mine.at[part], theirs.at[part], core_send.at[index], core_recv.at[index],
-            device_id=sibling, device_id_type=MESH)
-
-    def stream_across(d, c):
-        index = 1 + 2 * first_rows + d * chunks + c
+            mine.at[pl.ds(blocks, first)], every.at[pl.ds(stream_base(own_frame), first)],
+            core_send.at[index], core_recv.at[index], device_id=sibling, device_id_type=MESH)
+
+    def stream_across(c):
+        index = rows_here + 1 + c
         return pltpu.make_async_remote_copy(
-            landed.at[d, pl.ds(c * CHUNK, CHUNK)], theirs.at[pl.ds(stream_base[d] + first + c * CHUNK, CHUNK)],
+            landed.at[pl.ds(c * CHUNK, CHUNK)], every.at[pl.ds(stream_base(own_frame) + first + c * CHUNK, CHUNK)],
             core_send.at[index], core_recv.at[index], device_id=sibling, device_id_type=MESH)
 
     table_copy = pltpu.make_async_copy(columns_ref, table, local_sem.at[0])
-    rows_copy = pltpu.make_async_copy(columns_ref, table_rows, local_sem.at[1])
-    own_copy = pltpu.make_async_copy(values_ref, own, local_sem.at[2])
-    mine_copy = pltpu.make_async_copy(values_ref, mine.at[pl.ds(0, blocks)], local_sem.at[3])
-    table_copy.start()
-    rows_copy.start()
-    own_copy.start()
-    mine_copy.start()
+    lanes_copy = pltpu.make_async_copy(columns_ref, table_rows, local_sem.at[1])
+    rows_copy = pltpu.make_async_copy(values_ref, rows_own, local_sem.at[2])
+    own_copy = pltpu.make_async_copy(values_ref, own.at[:, halves[0], :], local_sem.at[3])
+    for copy in (table_copy, own_copy, lanes_copy, rows_copy):
+        copy.start()
 
     barrier = pltpu.get_barrier_semaphore()
-    for peer in (at(1), at(-1), sibling):
+    for peer in (behind, sibling):
         pl.semaphore_signal(barrier, inc=1, device_id=peer, device_id_type=MESH)
-    pl.semaphore_wait(barrier, 3)
-
+    pl.semaphore_wait(barrier, 2)
+
+    for r in reversed(range(rows_here)):
+        own_across(r).start()
     for n in range(first_rows):
-        for d in range(2):
-            unit_copy(d, n).start()
-    own_across().start()
-    mine[empty] = jnp.zeros((half, width), mine.dtype)
-    theirs[empty] = jnp.zeros((half, width), mine.dtype)
+        unit_copy(n, 0).start()
+    every[empty] = jnp.zeros((2 * half, width), every.dtype)
 
     table_copy.wait()
     zero = jnp.int32(0)
@@ -327,16 +333,20 @@
         value = jnp.where(value < 0, value + total_rows, value)
         return jnp.where(value >= total_rows, value - total_rows, value)
 
-    def distance(entry, i):
-        return (entry - i + REACH) & 31
-
-    @pl.loop(0, units * rows_here)
-    def _(n):
-        i = wrapped(first_row - HOPS * rows_here + n)
-        mask = zero
-        for k in range(slots):
-            mask = mask | (jnp.int32(1) << distance(table[k, i], i))
-        masks[n] = mask
+    def row_at(frame, r):
+        return wrapped(first_row + row_of(frame, r))
+
+    def distance(frame, entry, i):
+        return (jnp.where(frame == 0, entry - i, i - entry) + REACH) & 31
+
+    def fill_masks(frame):
+        @pl.loop(0, units * rows_here)
+        def _(n):
+            i = row_at(frame, n - HOPS * rows_here)
+            mask = zero
+            for k in range(slots):
+                mask = mask | (jnp.int32(1) << distance(frame, table[k, i], i))
+            masks[n] = mask
 
     def unit_mask(unit, r):
         return masks[rows_here * (unit + HOPS) + r]
@@ -350,105 +360,114 @@
                 got = got | jnp.where(((mask >> (step + REACH)) & 1) == 1, shifted_mask(mask, step), 0)
         return got
 
-    def needs_at(d, back, n, which):
-        return ((d * (HOPS + 1) + back) * rows_here + n) * 3 + which
-
-    def fill_needs(d, back):
-        sign = directions[d]
+    def needs_at(back, n, which):
+        return (back * rows_here + n) * 3 + which
+
+    def fill_needs(back):
         for n in range(rows_here):
-            r = row_of(d, n)
-            near, far, last = (need(-sign * back, sign * (away - back), r) for away in (1, 2, 3))
+            near, far, last = (need(-back, away - back, rows_here - 1 - n) for away in (1, 2, 3))
             for which, bits in enumerate((near | far | last, far | last, last)):
-                needs[needs_at(d, back, n, which)] = bits
-
-    def of_row(d, back, n):
-        r = row_of(d, n)
-        j = wrapped(first_row - directions[d] * back * rows_here + r)
-        wanted = [needs[needs_at(d, back, n, which)] for which in range(3)]
-        blocks_here = []
+                needs[needs_at(back, n, which)] = bits
+
+    def of_row(frame, back, n):
+        r = rows_here - 1 - n
+        j = row_at(frame, r - back * rows_here)
+        start = row_of(frame, r) * slots
+        wanted = [needs[needs_at(back, n, which)] for which in range(3)]
+        found = []
         for s in range(slots):
-            e = distance(table[s, j], j)
-            blocks_here.append((r * slots + s, *((bits >> e) & 1 for bits in wanted)))
-        return blocks_here
-
-    def count(d, back, which, rows):
+            e = distance(frame, table[s, j], j)
+            found.append((start + s, *((bits >> e) & 1 for bits in wanted)))
+        return found
+
+    def count(back, which, rows):
         total = zero
         for n in rows:
-            bits = needs[needs_at(d, back, n, which)] & unit_mask(-directions[d] * back, row_of(d, n))
-            total = total + ones(bits)
+            total = total + ones(needs[needs_at(back, n, which)] & unit_mask(-back, rows_here - 1 - n))
         return total
 
     firsts, tails = range(first_rows), range(first_rows, rows_here)
 
-    for d in range(2):
-        fill_needs(d, 0)
-
-        bits = zero
-        for n in tails:
-            for s, (_, near, _, _) in enumerate(of_row(d, 0, n)):
-                bits = bits | (near << ((n - first_rows) * slots + s))
-
-        def natural(found):
-            n = found // slots if d == 1 else 1 - found // slots
-            base = first if d == 1 else 0
-            return base + n * slots + lax.rem(found, slots)
-
-        def arrange(s, bits):
-            found, bits = lowest(bits, blocks - first)
-            order[d * STREAM + s] = natural(found)
-            return bits
-
-        lax.fori_loop(first, blocks, arrange, bits)
+    def natural(n, s):
+        return row_of(own_frame, rows_here - 1 - n) * slots + s
+
+    fill_masks(own_frame)
+    fill_needs(0)
+    bits = zero
+    for n in tails:
+        for s, (_, near, _, _) in enumerate(of_row(own_frame, 0, n)):
+            bits = bits | (near << ((n - first_rows) * slots + s))
+
+    def arrange_own(s, bits):
+        found, bits = lowest(bits, blocks - first)
+        order[s] = natural(first_rows + found // slots, lax.rem(found, slots))
+        return bits
+
+    lax.fori_loop(first, blocks, arrange_own, bits)
 
     own_copy.wait()
-
-    sends_short = seam_streams(col, cols_axis)
-    gets_short = seam_streams(lax.rem(col + cols_axis - 1, cols_axis), cols_axis)
-
-    def unless(short, d, c, step):
-        if d == 0 and first + c * CHUNK >= SEAM_STREAM:
+    for r in reversed(range(rows_here)):
+        own_across(r).wait_recv()
+        n = rows_here - 1 - r
+        if n < first_rows:
+            unit_copy(n, 1).start()
+    mine_copy = pltpu.make_async_copy(own, mine.at[pl.ds(0, blocks)], local_sem.at[4])
+    every_copy = pltpu.make_async_copy(own, every.at[pl.ds(0, blocks)], local_sem.at[5])
+    mine_copy.start()
+    every_copy.start()
+
+    right = layer == 0
+    sends_short = right & seam_streams(col, cols_axis)
+    seam_here = seam_streams(lax.rem(col + cols_axis - 1, cols_axis), cols_axis)
+    gets_short = right & seam_here
+    other_short = jnp.logical_not(right) & seam_here
+
+    def unless(short, c, step):
+        if first + c * CHUNK >= SEAM_STREAM:
             pl.when(jnp.logical_not(short))(step)
         else:
             step()
 
-    def pack(d, c, source):
+    def pack(c, source):
         def step():
             for s in range(c * CHUNK, (c + 1) * CHUNK):
-                packed[d, s] = source[order[d * STREAM + first + s]]
-            stream_copy(d, c).start()
-        unless(sends_short, d, c, step)
+                packed[s] = source[order[first + s]]
+            stream_copy(c).start()
+        unless(sends_short, c, step)
 
     for c in range(FIRST_LAG):
-        for d in range(2):
-            pack(d, c, own)
-
-    for d, sign in enumerate(directions):
+        pack(c, own)
+
+    def fill_slots(frame, with_order):
         for back in range(1, HOPS + 1):
-            fill_needs(d, back)
-        tail = [count(d, back, 0, tails) for back in range(HOPS + 1)]
-        far_first, far_tail = ([count(d, back, 1, rows) for back in range(HOPS + 1)] for rows in (firsts, tails))
-        last_first, last_tail = ([count(d, back, 2, rows) for back in range(HOPS + 1)] for rows in (firsts, tails))
+            fill_needs(back)
+        tail = [count(back, 0, tails) for back in range(HOPS + 1)]
+        far_first, far_tail = ([count(back, 1, rows) for back in range(HOPS + 1)] for rows in (firsts, tails))
+        last_first, last_tail = ([count(back, 2, rows) for back in range(HOPS + 1)] for rows in (firsts, tails))
 
         def starts(here):
             return layout(first, tail, far_first, far_tail, last_first, last_tail,
                           lambda counts, n: counts[min(here + n, HOPS)], jnp.maximum)
 
-        one, two, three, four, _ = starts(0)
         one_in, two_in, three_in, four_in, _ = starts(1)
-        base = stream_base[d]
+        base = stream_base(frame)
+
+        def unit_at(back):
+            return jnp.where(frame == 0, HOPS - back, HOPS + back) * blocks
 
         def note(back, block, spot):
-            slot_of[(HOPS - sign * back) * blocks + block] = base + jnp.clip(spot, 0, STREAM - 1)
+            slot_of[unit_at(back) + block] = base + jnp.clip(spot, 0, STREAM - 1)
 
         words = []
         seen = zero
         for rows in (firsts, tails):
             last_bits = far_bits = zero
             for n in rows:
-                for s, (block, near, far, last) in enumerate(of_row(d, 1, n)):
+                for s, (block, near, far, last) in enumerate(of_row(frame, 1, n)):
                     step = (n - rows[0]) * slots + s
-                    last_bits = last_bits | (last << step)
-                    far_bits = far_bits | ((far & (1 - last)) << step)
+                    if with_order:
+                        last_bits = last_bits | (last << step)
+                        far_bits = far_bits | ((far & (1 - last)) << step)
                     if rows is firsts:
                         note(1, block, step)
                     else:
@@ -459,13 +478,18 @@
         for rows, start, total, later in ((firsts, one_in, last_first[2], three_in), (tails, two_in, last_tail[2], four_in)):
             last_spot, far_spot, spot = start, start + total, later
             for n in rows:
-                for block, _, far, last in of_row(d, 2, n):
+                for block, _, far, last in of_row(frame, 2, n):
                     note(2, block, jnp.where(last == 1, last_spot, far_spot))
                     last_spot = last_spot + last
                     far_spot = far_spot + (far & (1 - last))
-                for block, _, _, last in of_row(d, 3, n):
+                for block, _, _, last in of_row(frame, 3, n):
                     note(3, block, spot)
                     spot = spot + last
+        if not with_order:
+            return
+
+        one, two, three, four, _ = starts(0)
+        unit_behind = unit_at(1)
 
         def arrange(with_own, s, carry):
             bits_one, bits_two, bits_three, bits_four = carry
@@ -474,22 +498,25 @@
             bits = jnp.where(from_first, jnp.where(use_last, bits_one, bits_two),
                              jnp.where(use_last, bits_three, bits_four))
             found, rest = lowest(bits, first)
-            n, r = found // slots, lax.rem(found, slots)
-            n = jnp.where(from_first, n, first_rows + n)
-            spot = slot_of[(HOPS - sign) * blocks + (rows_here - 1 - n if d == 0 else n) * slots + r]
-            spot = jnp.where(s >= three, base + one_in + s - three, spot)
-            spot = jnp.where(s >= four, base + two_in + s - four, spot)
-            spot = jnp.clip(spot, 0, empty)
+            n = jnp.where(from_first, 0, first_rows) + found // slots
+            spot = slot_of[unit_behind + natural(n, lax.rem(found, slots))] - base
+            spot = jnp.where(s >= three, one_in + s - three, spot)
+            spot = jnp.where(s >= four, two_in + s - four, spot)
+            spot = blocks + jnp.clip(spot, 0, STREAM - 1)
             active = True
             if with_own:
                 active = s >= one
-                spot = jnp.where(active, spot, order[d * STREAM + s])
-            order[d * STREAM + s] = spot
+                spot = jnp.where(active, spot, order[s])
+            order[s] = spot
             pick = [from_first & use_last, from_first & ~use_last, ~from_first & use_last, ~from_first & ~use_last]
             return tuple(jnp.where(p & active, rest, b) for p, b in zip(pick, carry))
 
         carry = lax.fori_loop(first + FIRST_LAG * CHUNK, blocks, functools.partial(arrange, True), tuple(words))
         lax.fori_loop(blocks, STREAM, functools.partial(arrange, False), carry)
+
+    fill_slots(own_frame, True)
+    fill_masks(other_frame)
+    fill_slots(other_frame, False)
 
     @pl.loop(0, blocks)
     def _(step):
@@ -509,45 +536,43 @@
             spot = slot_of[base + jnp.maximum(found, 0)]
             place[step * slots + m] = jnp.where(found < 0, empty, spot)
 
-    def take(d, c):
+    def take(c):
         def step():
-            stream_copy(d, c).wait_recv()
-            stream_across(d, c).start()
-            mine[pl.ds(stream_base[d] + first + c * CHUNK, CHUNK)] = landed[d, pl.ds(c * CHUNK, CHUNK)]
-        unless(gets_short, d, c, step)
+            stream_copy(c).wait_recv()
+            stream_across(c).start()
+            got = landed[pl.ds(c * CHUNK, CHUNK)]
+            mine[pl.ds(blocks + first + c * CHUNK, CHUNK)] = got
+            every[pl.ds(stream_base(own_frame) + first + c * CHUNK, CHUNK)] = got
+        unless(gets_short, c, step)
 
     mine_copy.wait()
     for n in range(first_rows):
-        for d in range(2):
-            unit_copy(d, n).wait_recv()
-            unit_across(d, n).start()
-
-    shares = 10
+        for which in range(2):
+            unit_copy(n, which).wait_recv()
+    unit_across().start()
+    unit_every = pltpu.make_async_copy(
+        mine.at[pl.ds(blocks, first)], every.at[pl.ds(stream_base(own_frame), first)], local_sem.at[6])
+    unit_every.start()
+
+    shares = blocks // CHUNK
     for c in range(FIRST_LAG, chunks):
-        for d in range(2):
-            if c >= LAG:
-                take(d, c - LAG)
-            pack(d, c, mine)
+        if c >= LAG:
+            take(c - LAG)
+        pack(c, mine)
         n = c - FIRST_LAG
         if n < shares:
             pl.loop(n * blocks // shares, (n + 1) * blocks // shares)(find)
+    lanes_copy.wait()
+    excess_ref[0, 0] = stream_excess(table_rows, total_rows, rows_here, cols_axis)
+    for c in range(chunks - LAG, chunks):
+        take(c)
+
     rows_copy.wait()
-    excess_ref[0, 0] = stream_excess(table_rows, total_rows, rows_here, cols_axis)
-    for t in range(rows_here):
-        for k in range(slots):
-            block = own[t * slots + k]
-            turned = jnp.concatenate([block[:, width // 2:], block[:, :width // 2]], axis=1)
-            left_side[t, :, k * width:(k + 1) * width] = jnp.where(layer == 0, block, turned)
-    for c in range(chunks - LAG, chunks):
-        for d in range(2):
-            take(d, c)
-
-    own_across().wait_recv()
-    for d in range(2):
-        for n in range(first_rows):
-            unit_across(d, n).wait_recv()
-        for c in range(chunks):
-            unless(gets_short, d, c, lambda d=d, c=c: stream_across(d, c).wait_recv())
+    every_copy.wait()
+    unit_every.wait()
+    unit_across().wait_recv()
+    for c in range(chunks):
+        unless(other_short, c, lambda c=c: stream_across(c).wait_recv())
 
     pairs = slots // 2
 
@@ -555,35 +580,36 @@
     def _(step):
         t, pair = step // pairs, lax.rem(step, pairs)
         start = t * slots * slots + 2 * pair
-
-        def block(index):
-            return jnp.concatenate([mine[index], theirs[index]], axis=0)
-
-        right = jnp.concatenate([
-            jnp.concatenate([block(place[start + k * slots]), block(place[start + k * slots + 1])], axis=1)
+        left = jnp.concatenate([rows_own[t * slots + k] for k in range(slots)], axis=1)
+        rhs = jnp.concatenate([
+            jnp.concatenate([every[place[start + k * slots]], every[place[start + k * slots + 1]]], axis=1)
             for k in range(slots)], axis=0)
-        product = jnp.dot(left_side[t], right, preferred_element_type=jnp.float32).astype(out_ref.dtype)
+        product = jnp.dot(left, rhs, preferred_element_type=jnp.float32).astype(out_ref.dtype)
         out_ref[t, 2 * pair] = product[:, :width]
         out_ref[t, 2 * pair + 1] = product[:, width:]
 
-    own_across().wait_send()
-    for d in range(2):
-        for n in range(first_rows):
-            unit_copy(d, n).wait_send()
-            unit_across(d, n).wait_send()
-        for c in range(chunks):
-            unless(sends_short, d, c, lambda d=d, c=c: stream_copy(d, c).wait_send())
-            unless(gets_short, d, c, lambda d=d, c=c: stream_across(d, c).wait_send())
+    for r in range(rows_here):
+        own_across(r).wait_send()
+    for n in range(first_rows):
+        for which in range(2):
+            unit_copy(n, which).wait_send()
+    unit_across().wait_send()
+    for c in range(chunks):
+        unless(sends_short, c, lambda c=c: stream_copy(c).wait_send())
+        unless(gets_short, c, lambda c=c: stream_across(c).wait_send())
 
 
 def sparse_square(sizes, table, values):
     rows_here, slots, half, width = values.shape
     blocks = rows_here * slots
     first_rows = rows_here // 2
-    spots = blocks + 2 * STREAM + 1
     units = 2 * HOPS + 1
     chunks = (STREAM - first_rows * slots) // CHUNK
-    crossings = 1 + 2 * first_rows + 2 * chunks
+    crossings = rows_here + 1 + chunks
+
+    def whole_blocks(count):
+        return pltpu.VMEM((count, 2 * half, width), values.dtype)
+
     return pl.pallas_call(
         functools.partial(sparse_kernel, sizes),
         out_shape=[jax.ShapeDtypeStruct(values.shape, values.dtype), jax.ShapeDtypeStruct((1, 1), jnp.int32)],
@@ -591,25 +617,25 @@
         out_specs=[pl.BlockSpec(memory_space=pltpu.VMEM), pl.BlockSpec(memory_space=pltpu.SMEM)],
         scratch_shapes=[
             pltpu.VMEM((blocks, half, width), values.dtype),
-            pltpu.VMEM((spots, half, width), values.dtype),
-            pltpu.VMEM((spots, half, width), values.dtype),
-            pltpu.VMEM((2, chunks * CHUNK, half, width), values.dtype),
-            pltpu.VMEM((2, chunks * CHUNK, half, width), values.dtype),
-            pltpu.VMEM((rows_here, half, slots * width), values.dtype),
+            whole_blocks(blocks),
+            whole_blocks(blocks + STREAM),
+            whole_blocks(blocks + 2 * STREAM + 1),
+            whole_blocks(chunks * CHUNK),
+            whole_blocks(chunks * CHUNK),
             pltpu.SMEM(table.shape, jnp.int32),
             pltpu.VMEM(table.shape, jnp.int32),
             pltpu.SMEM((units * rows_here,), jnp.int32),
-            pltpu.SMEM((2 * (HOPS + 1) * rows_here * 3,), jnp.int32),
-            pltpu.SMEM((2 * STREAM,), jnp.int32),
+            pltpu.SMEM(((HOPS + 1) * rows_here * 3,), jnp.int32),
+            pltpu.SMEM((STREAM,), jnp.int32),
             pltpu.SMEM((units * blocks,), jnp.int32),
             pltpu.SMEM((blocks * slots,), jnp.int32),
-            pltpu.SemaphoreType.DMA((2, first_rows)),
-            pltpu.SemaphoreType.DMA((2, first_rows)),
-            pltpu.SemaphoreType.DMA((2, chunks)),
-            pltpu.SemaphoreType.DMA((2, chunks)),
+            pltpu.SemaphoreType.DMA((first_rows, 2)),
+            pltpu.SemaphoreType.DMA((first_rows, 2)),
+            pltpu.SemaphoreType.DMA((chunks,)),
+            pltpu.SemaphoreType.DMA((chunks,)),
             pltpu.SemaphoreType.DMA((crossings,)),
             pltpu.SemaphoreType.DMA((crossings,)),
-            pltpu.SemaphoreType.DMA((4,)),
+            pltpu.SemaphoreType.DMA((7,)),
         ],
         compiler_params=pltpu.CompilerParams(
             collective_id=0, has_side_effects=True, vmem_limit_bytes=56 << 20),

time: 61.1 us -> 56.8 us (0.930)
  Pallas kernels: 59.5 us -> 55.1 us
    pallas_call x1, Pallas kernels: 59.5 us -> 55.1 us  [sparse_square(): pl.pallas_call(functools.partial(sparse_kernel, sizes), out_shape=[jax.Sh...]
where the time goes in v4:
time: 56.8 us; the launch traced here: 56.6 us
  Pallas kernels  55.1 us (97%)
  local copies, waits for them, and re-layouts  0.85 us (1%)
  between operations  0.65 us (1%)
    pallas_call x1, Pallas kernels, sparse_square(): pl.pallas_call(functools.partial(sparse_kernel, sizes), out_shape=[jax.Sh...  55.1 us

profile of v4, /device:TPU:1, one launch (start us, length us, event | category | flops | bytes accessed | tf_op | source)
XLA Modules:
  0.0 56.6 jit_solution(13969185248715240448)
XLA Ops:
  0.0 0.0 copy-start
  0.0 0.0 copy-start.1
  0.0 55.1 %sparse_square.1 = (bf16[4,10,64,128]{3,2,1,0:T(8,128)(2,1)S(1)}, s32[1,1]{1,0:T(1,128)}) custom-call(s32[10,1536]{1,0:T(8,128)} %bitcast.4, bf16[40,64,128]{2,1,0:T(8,128)(2,1)} %bitcast.3), custom_call_target="tpu_custom_call" | custom-call | tf_op jit(solution)/shard_map/sparse_square/pallas_call | solution.py:613
  55.7 0.0 copy-done
  55.7 0.0 copy-done.1
  55.8 0.8 %copy.8 = bf16[4,10,64,128]{3,2,1,0:T(8,128)(2,1)} copy(bf16[4,10,64,128]{3,2,1,0:T(8,128)(2,1)S(1)} %get-tuple-element.19) | data formatting | bytes 1310720
  (1 shorter events, 0.0 us)
Async XLA Ops:
  0.0 55.7 %copy-start = (bf16[4,10,64,128]{3,2,1,0:T(8,128)(2,1)S(1)}, bf16[4,10,64,128]{3,2,1,0:T(8,128)(2,1)}, u32[]{:S(2)}) copy-start(bf16[4,10,64,128]{3,2,1,0:T(8,128)(2,1)} %param.4) | copy-start | bytes 1966084
  0.0 55.7 %copy-start.1 = (s32[1536,10]{0,1:T(8,128)S(1)}, s32[1536,10]{0,1:T(8,128)}, u32[]{:S(2)}) copy-start(s32[1536,10]{0,1:T(8,128)} %param.5) | copy-start | bytes 184324

commit v5 on v4

--- a/solution.py
+++ b/solution.py
@@ -11,10 +11,10 @@
 REACH = 12
 SPAN = 2 * REACH
 STREAM = 92
-SEAM_STREAM = 78
-CHUNK = 2
-LAG = 7
-FIRST_LAG = 6
+SEAM_STREAM = 80
+CHUNK = 4
+LAG = 4
+FIRST_LAG = 3
 MESH = pl.DeviceIdType.MESH
 
 
@@ -155,7 +155,7 @@
 
 
 def seam_streams(col, cols_axis):
-    return (col >= cols_axis - 1) | (col <= 1)
+    return (col >= cols_axis - 1) | (col <= 3)
 
 
 def layout(first, tail, far_first, far_tail, last_first, last_tail, behind, larger):
@@ -258,13 +258,13 @@
     chunks = (STREAM - first) // CHUNK
     units = 2 * HOPS + 1
     empty = blocks + 2 * STREAM
-    own_frame, other_frame = layer, 1 - layer
+    own_frame, other_frame = 1 - layer, layer
 
     def at(offset):
         there = lax.rem(position + offset + positions, positions)
         return (there // cols_axis, lax.rem(there, cols_axis), layer)
 
-    ahead, behind = at(1 - 2 * layer), at(2 * layer - 1)
+    ahead, behind = at(1 - 2 * own_frame), at(2 * own_frame - 1)
     sibling = (row, col, 1 - layer)
     halves = [pl.ds(pl.multiple_of(which * half, half), half) for which in (layer, 1 - layer)]
 
@@ -320,10 +320,11 @@
         pl.semaphore_signal(barrier, inc=1, device_id=peer, device_id_type=MESH)
     pl.semaphore_wait(barrier, 2)
 
-    for r in reversed(range(rows_here)):
-        own_across(r).start()
     for n in range(first_rows):
         unit_copy(n, 0).start()
+        own_across(rows_here - 1 - n).start()
+    for r in reversed(range(rows_here - first_rows)):
+        own_across(r).start()
     every[empty] = jnp.zeros((2 * half, width), every.dtype)
 
     table_copy.wait()
@@ -416,7 +417,7 @@
     mine_copy.start()
     every_copy.start()
 
-    right = layer == 0
+    right = own_frame == 0
     sends_short = right & seam_streams(col, cols_axis)
     seam_here = seam_streams(lax.rem(col + cols_axis - 1, cols_axis), cols_axis)
     gets_short = right & seam_here
@@ -564,6 +565,20 @@
             pl.loop(n * blocks // shares, (n + 1) * blocks // shares)(find)
     lanes_copy.wait()
     excess_ref[0, 0] = stream_excess(table_rows, total_rows, rows_here, cols_axis)
+    def wait_sends(start, end):
+        for c in range(start, end):
+            unless(sends_short, c, lambda c=c: stream_copy(c).wait_send())
+            unless(gets_short, c, lambda c=c: stream_across(c).wait_send())
+
+    early_chunks = (SEAM_STREAM - first) // CHUNK - 2 * LAG
+    for r in range(rows_here):
+        own_across(r).wait_send()
+    for n in range(first_rows):
+        for which in range(2):
+            unit_copy(n, which).wait_send()
+    unit_across().wait_send()
+    wait_sends(0, early_chunks)
+
     for c in range(chunks - LAG, chunks):
         take(c)
 
@@ -576,7 +591,7 @@
 
     pairs = slots // 2
 
-    @pl.loop(0, rows_here * pairs, unroll=5)
+    @pl.loop(0, rows_here * pairs, unroll=20)
     def _(step):
         t, pair = step // pairs, lax.rem(step, pairs)
         start = t * slots * slots + 2 * pair
@@ -588,15 +603,7 @@
         out_ref[t, 2 * pair] = product[:, :width]
         out_ref[t, 2 * pair + 1] = product[:, width:]
 
-    for r in range(rows_here):
-        own_across(r).wait_send()
-    for n in range(first_rows):
-        for which in range(2):
-            unit_copy(n, which).wait_send()
-    unit_across().wait_send()
-    for c in range(chunks):
-        unless(sends_short, c, lambda c=c: stream_copy(c).wait_send())
-        unless(gets_short, c, lambda c=c: stream_across(c).wait_send())
+    wait_sends(early_chunks, chunks)
 
 
 def sparse_square(sizes, table, values):

time: 56.8 us -> 55 us (0.968)
  Pallas kernels: 55.1 us -> 53.4 us
    pallas_call x1, Pallas kernels: 55.1 us -> 53.4 us  [sparse_square(): pl.pallas_call(functools.partial(sparse_kernel, sizes), out_shape=[jax.Sh...]
where the time goes in v5:
time: 55 us; the launch traced here: 54.9 us
  Pallas kernels  53.4 us (97%)
  local copies, waits for them, and re-layouts  0.85 us (2%)
  between operations  0.65 us (1%)
    pallas_call x1, Pallas kernels, sparse_square(): pl.pallas_call(functools.partial(sparse_kernel, sizes), out_shape=[jax.Sh...  53.4 us

profile of v5, /device:TPU:1, one launch (start us, length us, event | category | flops | bytes accessed | tf_op | source)
XLA Modules:
  0.0 54.9 jit_solution(16914138758236468834)
XLA Ops:
  0.0 0.0 copy-start
  0.0 0.0 copy-start.1
  0.0 53.4 %sparse_square.1 = (bf16[4,10,64,128]{3,2,1,0:T(8,128)(2,1)S(1)}, s32[1,1]{1,0:T(1,128)}) custom-call(s32[10,1536]{1,0:T(8,128)} %bitcast.4, bf16[40,64,128]{2,1,0:T(8,128)(2,1)} %bitcast.3), custom_call_target="tpu_custom_call" | custom-call | tf_op jit(solution)/shard_map/sparse_square/pallas_call | solution.py:620
  54.0 0.0 copy-done
  54.0 0.0 copy-done.1
  54.1 0.8 %copy.8 = bf16[4,10,64,128]{3,2,1,0:T(8,128)(2,1)} copy(bf16[4,10,64,128]{3,2,1,0:T(8,128)(2,1)S(1)} %get-tuple-element.19) | data formatting | bytes 1310720
  (1 shorter events, 0.0 us)
Async XLA Ops:
  0.0 54.0 %copy-start = (bf16[4,10,64,128]{3,2,1,0:T(8,128)(2,1)S(1)}, bf16[4,10,64,128]{3,2,1,0:T(8,128)(2,1)}, u32[]{:S(2)}) copy-start(bf16[4,10,64,128]{3,2,1,0:T(8,128)(2,1)} %param.4) | copy-start | bytes 1966084
  0.0 54.0 %copy-start.1 = (s32[1536,10]{0,1:T(8,128)S(1)}, s32[1536,10]{0,1:T(8,128)}, u32[]{:S(2)}) copy-start(s32[1536,10]{0,1:T(8,128)} %param.5) | copy-start | bytes 184324

commit v6 on v5

--- a/solution.py
+++ b/solution.py
@@ -542,7 +542,8 @@
             stream_copy(c).wait_recv()
             stream_across(c).start()
             got = landed[pl.ds(c * CHUNK, CHUNK)]
-            mine[pl.ds(blocks + first + c * CHUNK, CHUNK)] = got
+            if c < chunks - LAG:
+                mine[pl.ds(blocks + first + c * CHUNK, CHUNK)] = got
             every[pl.ds(stream_base(own_frame) + first + c * CHUNK, CHUNK)] = got
         unless(gets_short, c, step)
 
@@ -578,15 +579,17 @@
             unit_copy(n, which).wait_send()
     unit_across().wait_send()
     wait_sends(0, early_chunks)
-
-    for c in range(chunks - LAG, chunks):
-        take(c)
-
     rows_copy.wait()
     every_copy.wait()
     unit_every.wait()
     unit_across().wait_recv()
-    for c in range(chunks):
+    for c in range(early_chunks):
+        unless(other_short, c, lambda c=c: stream_across(c).wait_recv())
+
+    for c in range(chunks - LAG, chunks):
+        take(c)
+
+    for c in range(early_chunks, chunks):
         unless(other_short, c, lambda c=c: stream_across(c).wait_recv())
 
     pairs = slots // 2

time: 55 us -> 55 us (level)
  no operation moved by 1% of the time
where the time goes in v6:
time: 55 us; the launch traced here: 54.9 us
  Pallas kernels  53.4 us (97%)
  local copies, waits for them, and re-layouts  0.85 us (2%)
  between operations  0.65 us (1%)
    pallas_call x1, Pallas kernels, sparse_square(): pl.pallas_call(functools.partial(sparse_kernel, sizes), out_shape=[jax.Sh...  53.4 us

profile of v6, /device:TPU:1, one launch (start us, length us, event | category | flops | bytes accessed | tf_op | source)
XLA Modules:
  0.0 54.9 jit_solution(3425258576774439602)
XLA Ops:
  0.0 0.0 copy-start
  0.0 0.0 copy-start.1
  0.0 53.4 %sparse_square.1 = (bf16[4,10,64,128]{3,2,1,0:T(8,128)(2,1)S(1)}, s32[1,1]{1,0:T(1,128)}) custom-call(s32[10,1536]{1,0:T(8,128)} %bitcast.4, bf16[40,64,128]{2,1,0:T(8,128)(2,1)} %bitcast.3), custom_call_target="tpu_custom_call" | custom-call | tf_op jit(solution)/shard_map/sparse_square/pallas_call | solution.py:623
  54.0 0.0 copy-done
  54.0 0.0 copy-done.1
  54.0 0.8 %copy.8 = bf16[4,10,64,128]{3,2,1,0:T(8,128)(2,1)} copy(bf16[4,10,64,128]{3,2,1,0:T(8,128)(2,1)S(1)} %get-tuple-element.19) | data formatting | bytes 1310720
  (1 shorter events, 0.0 us)
Async XLA Ops:
  0.0 54.0 %copy-start = (bf16[4,10,64,128]{3,2,1,0:T(8,128)(2,1)S(1)}, bf16[4,10,64,128]{3,2,1,0:T(8,128)(2,1)}, u32[]{:S(2)}) copy-start(bf16[4,10,64,128]{3,2,1,0:T(8,128)(2,1)} %param.4) | copy-start | bytes 1966084
  0.0 54.0 %copy-start.1 = (s32[1536,10]{0,1:T(8,128)S(1)}, s32[1536,10]{0,1:T(8,128)}, u32[]{:S(2)}) copy-start(s32[1536,10]{0,1:T(8,128)} %param.5) | copy-start | bytes 184324
